TPU v7x, 512 devices: a whole 4x8x8 slice. The times are simulated.
512 devices in a mesh: gx: 8 (over y_hi, core), yz: 64 (over z, x, y_lo).
Axes of the slice: x: 4, y: 8 (y_hi: 4, y_lo: 2; y = y_hi * 2 + y_lo), z: 8, core: 2. Of those that a mesh axis runs over, the one named last changes fastest.
Arguments:
- snapshot: float32 [1024, 65536], P('gx', 'yz'), may hold values from -40 to 40, as said below
- start: float32 [1024, 192], replicated, may hold values from -6 to 6
Outputs:
- basis: float32 [1024, 192], P('gx')
- projected: float32 [1024, 65536], P('gx', 'yz')
Inputs may be any that keep to these rules, and one draw needn't show every extreme that they name: Each x row of the snapshot has its own scale between 1 and 10; entries are independent.
All inputs are finite; a program needn't handle non-finite values.
Results may differ from a plain program's by a relative error of at most 0.00022.
Values sent between devices are 32-bit elements; how exact they have to be, the bound alone decides.
A program may use at most 64 MiB of HBM per device.

v0:
```python
import jax
import jax.numpy as jnp
from jax import lax
from jax.sharding import PartitionSpec as P

ITERS = 4


def body(snapshot, start):
    highest = lax.Precision.HIGHEST
    x_rows = snapshot.shape[0]
    all_cells = snapshot.shape[1] * lax.axis_size("yz")
    gathered = lax.all_gather(snapshot, "gx", axis=0, tiled=True)
    gram_part = jnp.dot(snapshot, gathered.T, precision=highest) / all_cells
    gram_block = lax.psum(gram_part, "yz")
    gram = lax.all_gather(gram_block, "gx", axis=0, tiled=True)
    basis_full = start
    for step in range(ITERS):
        image = jnp.dot(gram, basis_full, precision=highest)
        inner = jnp.dot(image.T, image, precision=highest)
        lower = jnp.linalg.cholesky(inner)
        basis_full = jax.scipy.linalg.solve_triangular(lower, image.T, lower=True).T
    offset = lax.axis_index("gx") * x_rows
    basis_mine = lax.dynamic_slice_in_dim(basis_full, offset, x_rows, 0)
    core = jnp.dot(basis_full.T, gathered, precision=highest)
    projected = jnp.dot(basis_mine, core, precision=highest)
    return (basis_mine, projected)


def solution(mesh):
    in_specs = (P("gx", "yz"), P())
    out_specs = (P("gx", None), P("gx", "yz"))
    return jax.shard_map(body, mesh=mesh, in_specs=in_specs, out_specs=out_specs, check_vma=False)
```

profile of v0, /device:TPU:1, one launch (start us, length us, event | category | flops | bytes accessed | tf_op | source)
XLA Modules:
  0.0 989.6 jit_solution(14868789026729008459)
XLA Ops:
  8.0 61.7 %all-gather.3.cloned.1.call-done = f32[1024,1024]{1,0:T(8,128)} async-done(((f32[128,1024]{1,0:T(8,128)}), f32[1024,1024]{1,0:T(8,128)}) %all-gather.3.cloned.1.call-update) | async-done | bytes 4194320 | tf_op jit(solution)/shard_map/all_gather | solution.py:13
  69.7 7.5 convolution_multiply_fusion
  77.5 565.5 %all-reduce.5.cloned.1.call-done = f32[128,1024]{1,0:T(8,128)} async-done(((f32[128,1024]{1,0:T(8,128)}), f32[128,1024]{1,0:T(8,128)}) %all-reduce.5.cloned.1.call-update) | async-done | bytes 524304 | tf_op jit(solution)/shard_map/psum | solution.py:15
  643.0 95.3 %all-gather.5.cloned.1.call-done = f32[1024,1024]{1,0:T(8,128)} async-done(((f32[128,1024]{1,0:T(8,128)}), f32[1024,1024]{1,0:T(8,128)}) %all-gather.5.cloned.1.call-update) | async-done | bytes 4194320 | tf_op jit(solution)/shard_map/all_gather | solution.py:16
  738.4 6.4 fusion.63
  745.7 11.7 %cholesky.228 = f32[128,128]{1,0:T(8,128)S(1)} custom-call(f32[128,128]{1,0:T(8,128)S(1)} %cholesky.376), custom_call_target="Cholesky" | custom-call | tf_op jit(solution)/shard_map/jit(cholesky)/cholesky | solution.py:21
  757.5 9.8 custom-call.17
  767.7 5.8 cholesky.248
  776.3 20.1 %custom-call.18 = f32[2,128,128]{1,2,0:T(8,128)S(1)} custom-call(f32[2,128,128]{2,1,0:T(8,128)S(1)} %pad_maximum_fusion.2), custom_call_target="InvertDiagBlocksLowerTriangular" | custom-call | tf_op jit(solution)/shard_map/jit(_solve_triangular)/triangular_solve | solution.py:22
  797.9 6.4 fusion.1
  805.3 11.7 %cholesky.266 = f32[128,128]{1,0:T(8,128)S(1)} custom-call(f32[128,128]{1,0:T(8,128)S(1)} %cholesky.379), custom_call_target="Cholesky" | custom-call | tf_op jit(solution)/shard_map/jit(cholesky)/cholesky | solution.py:21
  817.1 9.8 custom-call.19
  827.3 5.8 cholesky.286
  835.9 19.7 %custom-call.20 = f32[2,128,128]{1,2,0:T(8,128)S(1)} custom-call(f32[2,128,128]{2,1,0:T(8,128)S(1)} %pad_maximum_fusion.3), custom_call_target="InvertDiagBlocksLowerTriangular" | custom-call | tf_op jit(solution)/shard_map/jit(_solve_triangular)/triangular_solve | solution.py:22
  857.1 6.6 fusion.5
  864.7 11.7 %cholesky.304 = f32[128,128]{1,0:T(8,128)S(1)} custom-call(f32[128,128]{1,0:T(8,128)S(1)} %cholesky.382), custom_call_target="Cholesky" | custom-call | tf_op jit(solution)/shard_map/jit(cholesky)/cholesky | solution.py:21
  876.4 9.8 custom-call.21
  886.6 5.8 cholesky.324
  895.2 19.7 %custom-call.22 = f32[2,128,128]{1,2,0:T(8,128)S(1)} custom-call(f32[2,128,128]{2,1,0:T(8,128)S(1)} %pad_maximum_fusion.4), custom_call_target="InvertDiagBlocksLowerTriangular" | custom-call | tf_op jit(solution)/shard_map/jit(_solve_triangular)/triangular_solve | solution.py:22
  916.4 6.6 fusion.9
  924.0 11.7 %cholesky.342 = f32[128,128]{1,0:T(8,128)S(1)} custom-call(f32[128,128]{1,0:T(8,128)S(1)} %cholesky.385), custom_call_target="Cholesky" | custom-call | tf_op jit(solution)/shard_map/jit(cholesky)/cholesky | solution.py:21
  935.8 9.8 custom-call.23
  946.0 5.8 cholesky.362
  954.6 19.7 %custom-call.24 = f32[2,128,128]{1,2,0:T(8,128)S(1)} custom-call(f32[2,128,128]{2,1,0:T(8,128)S(1)} %pad_maximum_fusion.5), custom_call_target="InvertDiagBlocksLowerTriangular" | custom-call | tf_op jit(solution)/shard_map/jit(_solve_triangular)/triangular_solve | solution.py:22
  (88 shorter events, 25.2 us)
Async XLA Ops:
  7.2 731.2 %copy-start = (f32[1024,192]{0,1:T(8,128)S(1)}, f32[1024,192]{0,1:T(8,128)}, u32[]{:S(2)}) copy-start(f32[1024,192]{0,1:T(8,128)} %param.6) | copy-start | bytes 2359300
  7.2 62.5 %all-gather.3.cloned.1.call-start = ((), (), s32[]{:S(2)}) async-start(), calls=%async_computation | async-start | bytes 4718592 | tf_op jit(solution)/shard_map/all_gather | solution.py:13
  7.9 635.1 %all-reduce.5.cloned.1.call-start = ((), (), s32[]{:S(2)}) async-start(), calls=%async_computation.1 | async-start | bytes 1048576 | tf_op jit(solution)/shard_map/psum | solution.py:15
  77.3 661.1 %all-gather.5.cloned.1.call-start = ((), (), s32[]{:S(2)}) async-start(), calls=%async_computation.2 | async-start | bytes 4718592 | tf_op jit(solution)/shard_map/all_gather | solution.py:16
Sparse Core Ops, SparseCore 0:
  10.2 59.4 all-gather.2
  77.4 565.5 all-reduce.4
  645.4 92.9 all-gather.4
where the time goes:
time: 994 us; the launch traced here: 990 us
  waiting for transfers between devices  723 us (73%)
  other arithmetic  195 us (20%)
  matrix products  50.5 us (5%)
  between operations  19.8 us (2%)
    psum x1, waiting for transfers between devices, body(): gram_block = lax.psum(gram_part, 'yz')  566 us
    another operation x28, other arithmetic, body(): lower = jnp.linalg.cholesky(inner)  115 us
    all_gather x1, waiting for transfers between devices, body(): gram = lax.all_gather(gram_block, 'gx', axis=0, tiled=True)  95.3 us
    another operation x18, other arithmetic, body(): basis_full = jax.scipy.linalg.solve_triangular(lower, image.T, lower=True).T  79.6 us
    all_gather x1, waiting for transfers between devices, body(): gathered = lax.all_gather(snapshot, 'gx', axis=0, tiled=True)  61.7 us
    dot_general x4, matrix products, body(): image = jnp.dot(gram, basis_full, precision=highest)  26 us
  transfers between devices with their start and end apart: 3, of which 3 were waited for; matrix products, arithmetic and copies ran while one was open for 0% of the time, Pallas kernels for 0%

commit v1 on v0

v1 whole, which is shorter than its diff:
```python
import functools
import jax
import jax.numpy as jnp
from jax import lax
from jax.experimental import pallas as pl
from jax.experimental.pallas import tpu as pltpu
from jax.sharding import PartitionSpec as P

ITERS = 4
G, NYH, NZ, NX, NYL = 8, 4, 8, 4, 2
ROWS = 128
NB = 5
XROWS = NB * ROWS // NX
ZROWS = 24
PAD = NZ * ZROWS
N = 1024
RANK = 192
PANEL = 32
GROUP = 4
f32, bf16 = jnp.float32, jnp.bfloat16
MESH = pl.DeviceIdType.MESH


def split2(a):
    hi = a.astype(jnp.bfloat16)
    lo = (a - hi.astype(jnp.float32)).astype(jnp.bfloat16)
    return hi, lo


def dot_nt(a, b):
    return lax.dot_general(a, b, (((1,), (1,)), ((), ())), preferred_element_type=jnp.float32)


def gram_kernel(cells, s_ref, d_ref, f_ref, lhs, parts, xin, xsum, zin, zsum, yin, send, recv, local):
    g = lax.axis_index("gx")
    q = lax.axis_index("yz")
    yh, core = g // 2, g % 2
    z, x, yl = q // (NX * NYL), (q // NYL) % NX, q % NYL

    def gx_at(yh2, core2):
        return yh2 * 2 + core2

    def yz_at(z2, x2, yl2):
        return (z2 * NX + x2) * NYL + yl2

    pair = (gx_at(yh, 1 - core), q)
    up = [(gx_at((yh + k) % NYH, core), q) for k in range(NYH)]
    xs = [(g, yz_at(z, (x + k) % NX, yl)) for k in range(NX)]
    zs = [(g, yz_at((z + k) % NZ, x, yl)) for k in range(NZ)]
    ylo = (g, yz_at(z, x, 1 - yl))
    peers = [pair] + up[1:] + xs[1:] + zs[1:] + [ylo]

    barrier = pltpu.get_barrier_semaphore()
    for peer in peers:
        pl.semaphore_signal(barrier, inc=1, device_id=peer, device_id_type=MESH)
    pl.semaphore_wait(barrier, len(peers))

    sent = []
    count = [0]

    def slot():
        count[0] += 1
        return count[0] - 1

    def copy(src, dst, index, target):
        return pltpu.make_async_remote_copy(
            src_ref=src, dst_ref=dst, send_sem=send.at[index], recv_sem=recv.at[index],
            device_id=target, device_id_type=MESH)

    def push(src, dst, index, target):
        op = copy(src, dst, index, target)
        op.start()
        sent.append(op)

    def arrived(dst, index):
        copy(dst, dst, index, pair).wait_recv()

    half = ROWS // 2

    def chunk(block, c):
        return d_ref.at[block, pl.ds(c * half, half), :]

    s_own, s_right, s_left, s_opp = slot(), [slot(), slot()], [slot(), slot()], [slot(), slot()]
    s_pair = {(k, c): slot() for k in range(3) for c in range(2)}
    right, left = up[1], up[3]
    g_left, g_right, g_opp = left[0], right[0], up[2][0]
    for c in (0, 1):
        push(s_ref.at[pl.ds(c * half, half), :], chunk(g, c), s_right[c], right)
        push(s_ref.at[pl.ds((1 - c) * half, half), :], chunk(g, 1 - c), s_left[1 - c], left)
    push(s_ref, d_ref.at[g], s_own, pair)
    mine = pltpu.make_async_copy(s_ref, d_ref.at[g], local)
    mine.start()

    hi, lo = split2(s_ref[...])
    lhs[pl.ds(0, ROWS), :] = hi
    lhs[pl.ds(ROWS, ROWS), :] = lo
    mine.wait()

    arrived(chunk(g_left, 0), s_right[0])
    push(chunk(g_left, 0), chunk(g_left, 0), s_opp[0], right)
    push(chunk(g_left, 0), chunk(g_left, 0), s_pair[0, 0], pair)
    arrived(chunk(g_right, 1), s_left[1])
    push(chunk(g_right, 1), chunk(g_right, 1), s_opp[1], left)
    push(chunk(g_right, 1), chunk(g_right, 1), s_pair[1, 1], pair)
    arrived(chunk(g_left, 1), s_right[1])
    push(chunk(g_left, 1), chunk(g_left, 1), s_pair[0, 1], pair)
    arrived(chunk(g_right, 0), s_left[0])
    push(chunk(g_right, 0), chunk(g_right, 0), s_pair[1, 0], pair)
    arrived(chunk(g_opp, 0), s_opp[0])
    push(chunk(g_opp, 0), chunk(g_opp, 0), s_pair[2, 0], pair)
    arrived(chunk(g_opp, 1), s_opp[1])
    push(chunk(g_opp, 1), chunk(g_opp, 1), s_pair[2, 1], pair)
    other = pair[0]
    arrived(d_ref.at[other], s_own)
    for k, step in enumerate((3, 1, 2)):
        block = gx_at((yh + step) % NYH, 1 - core)
        for c in range(2):
            arrived(chunk(block, c), s_pair[k, c])

    for d in range(NB):
        b_hi, b_lo = split2(d_ref[(g + d) % G])
        both = dot_nt(lhs[...], b_hi)
        part = both[:ROWS] + both[ROWS:] + dot_nt(lhs[pl.ds(0, ROWS), :], b_lo)
        part = part * (1.0 / cells)
        for k in range(NX):
            parts[k, pl.ds(32 * d, 32), :] = part[32 * k:32 * k + 32]

    s_x = [slot() for _ in range(NX - 1)]
    for k in range(1, NX):
        push(parts.at[(x + k) % NX], xin.at[k - 1], s_x[k - 1], xs[k])
    xsum[pl.ds(XROWS, PAD - XROWS), :] = jnp.zeros((PAD - XROWS, 128), jnp.float32)
    total = parts[x]
    for k in range(1, NX):
        arrived(xin.at[k - 1], s_x[k - 1])
        total += xin[k - 1]
    xsum[pl.ds(0, XROWS), :] = total

    def z_rows(z2):
        return pl.ds(pl.multiple_of(z2 * ZROWS, 8), ZROWS)

    s_z = [slot() for _ in range(NZ - 1)]
    for k in range(1, NZ):
        push(xsum.at[z_rows((z + k) % NZ), :], zin.at[k - 1], s_z[k - 1], zs[k])
    total = xsum[z_rows(z), :]
    for k in range(1, NZ):
        arrived(zin.at[k - 1], s_z[k - 1])
        total += zin[k - 1]
    zsum[...] = total
    s_yl = slot()
    push(zsum, yin, s_yl, ylo)
    arrived(yin, s_yl)
    f_ref[core, x, yh, z_rows(z), :] = zsum[...] + yin[...]

    s_ay = [slot() for _ in range(NYH - 1)]
    for k in range(1, NYH):
        block = f_ref.at[core, x, yh, z_rows(z), :]
        push(block, block, s_ay[k - 1], up[k])
    for k in range(1, NYH):
        arrived(f_ref.at[core, x, (yh - k + NYH) % NYH, z_rows(z), :], s_ay[k - 1])
    s_az = [slot() for _ in range(NZ - 1)]
    for k in range(1, NZ):
        block = f_ref.at[core, x, :, z_rows(z), :]
        push(block, block, s_az[k - 1], zs[k])
    for k in range(1, NZ):
        arrived(f_ref.at[core, x, :, z_rows((z - k + NZ) % NZ), :], s_az[k - 1])

    def x_block(core2, x2):
        return f_ref.at[core2, x2, :, pl.ds(0, XROWS), :]

    s_ax = [slot() for _ in range(NX - 1)]
    s_ap = [slot() for _ in range(NX)]
    for k in range(1, NX):
        push(x_block(core, x), x_block(core, x), s_ax[k - 1], xs[k])
    push(x_block(core, x), x_block(core, x), s_ap[0], pair)
    for k in range(1, NX):
        x2 = (x - k + NX) % NX
        arrived(x_block(core, x2), s_ax[k - 1])
        push(x_block(core, x2), x_block(core, x2), s_ap[k], pair)
    for k in range(NX):
        arrived(x_block(1 - core, (x - k + NX) % NX), s_ap[k])
    for op in sent:
        op.wait_send()


SLOTS = 13 + 3 + 7 + 1 + 3 + 7 + 3 + 4


def gather_and_gram(snapshot, all_cells):

    cols = snapshot.shape[1]
    f32 = jnp.float32
    return pl.pallas_call(
        functools.partial(gram_kernel, all_cells),
        out_shape=(jax.ShapeDtypeStruct((G, ROWS, cols), f32),
                   jax.ShapeDtypeStruct((2, NX, NYH, PAD, 128), f32)),
        in_specs=[pl.BlockSpec(memory_space=pltpu.VMEM)],
        out_specs=(pl.BlockSpec(memory_space=pltpu.VMEM), pl.BlockSpec(memory_space=pltpu.VMEM)),
        scratch_shapes=[
            pltpu.VMEM((2 * ROWS, cols), jnp.bfloat16),
            pltpu.VMEM((NX, XROWS, 128), f32),
            pltpu.VMEM((NX - 1, XROWS, 128), f32),
            pltpu.VMEM((PAD, 128), f32),
            pltpu.VMEM((NZ - 1, ZROWS, 128), f32),
            pltpu.VMEM((ZROWS, 128), f32),
            pltpu.VMEM((ZROWS, 128), f32),
            pltpu.SemaphoreType.DMA((SLOTS,)),
            pltpu.SemaphoreType.DMA((SLOTS,)),
            pltpu.SemaphoreType.DMA,
        ],
        compiler_params=pltpu.CompilerParams(
            collective_id=0, has_side_effects=True, vmem_limit_bytes=40 * 2**20),
    )(snapshot)


def dot(a, b):
    return lax.dot_general(a, b, (((1,), (0,)), ((), ())), preferred_element_type=f32)


def dot3(a, b_hi, b_lo, nt=False):
    d = dot_nt if nt else dot
    m = a.shape[0]
    a_hi, a_lo = split2(a)
    both = d(jnp.concatenate([a_hi, a_lo], axis=0), b_hi)
    return both[:m] + (both[m:] + d(a_hi, b_lo))


def inverse_factor(m, w_ref):
    n = RANK
    lanes = lax.broadcasted_iota(jnp.int32, (1, n), 1)
    rest = m
    for p0 in range(0, n, PANEL):
        a = rest[:PANEL]
        rest = rest[PANEL:]
        below = rest
        rows = lax.broadcasted_iota(jnp.int32, (PANEL, n), 0)
        for k0 in range(0, PANEL, GROUP):
            c0 = p0 + k0
            ks = range(GROUP)
            cols = [jnp.broadcast_to(a[:, c0 + j:c0 + j + 1], (PANEL, n)) for j in ks]
            pivot = [[cols[j][k0 + i:k0 + i + 1] for j in ks] for i in ks]
            in_group = (lanes >= c0) & (lanes < c0 + GROUP)
            r = [jnp.where(in_group, jnp.where(lanes == c0 + j, 1.0, 0.0), a[k0 + j:k0 + j + 1]) for j in ks]
            inv = [None] * GROUP
            for j in ks:
                inv[j] = 1.0 / pivot[j][j]
                for i in range(j + 1, GROUP):
                    l = pivot[i][j] * inv[j]
                    r[i] = r[i] - l * r[j]
                    for t in range(j + 1, GROUP):
                        pivot[i][t] = pivot[i][t] - l * pivot[j][t]
            for j in ks:
                w_ref[c0 + j:c0 + j + 1, :] = jnp.where(lanes <= c0 + j, r[j] * lax.rsqrt(pivot[j][j]), 0.0)
            zs = [None] * GROUP
            for j in reversed(ks):
                t = r[j]
                for i in range(j + 1, GROUP):
                    t = t - pivot[j][i] * zs[i]
                zs[j] = t * inv[j]
            a = jnp.where(in_group, 0.0, a)
            for j in ks:
                a = a - cols[j] * zs[j]
            for j in ks:
                a = jnp.where(rows == k0 + j, zs[j], a)
        if p0 + PANEL < n:
            tile = p0 // 128 * 128
            width = min(128, n - tile)
            pad = [jnp.zeros((p0 - tile, n), f32)] if p0 > tile else []
            after = tile + width - p0 - PANEL
            pad_after = [jnp.zeros((after, n), f32)] if after else []
            z_hi, z_lo = split2(jnp.concatenate(pad + [a] + pad_after, axis=0))
            in_panel = (lanes >= p0) & (lanes < p0 + PANEL)
            rest = jnp.where(in_panel, 0.0, below) - dot3(below[:, tile:tile + width], z_hi, z_lo)


def iterate_kernel(d_ref, f_ref, start_ref, basis_ref, out_ref, g_hi, g_lo, q_ref, w_ref):
    g = lax.axis_index("gx")
    for i in range(G):
        for d in range(NB):
            j = (i + d) % G
            block = jnp.concatenate(
                [f_ref[i % 2, k, i // 2, 32 * d:32 * d + 32, :] for k in range(NX)], axis=0)
            hi, lo = split2(block)
            g_hi[ROWS * i:ROWS * (i + 1), ROWS * j:ROWS * (j + 1)] = hi
            g_lo[ROWS * i:ROWS * (i + 1), ROWS * j:ROWS * (j + 1)] = lo
            if 0 < d < NB - 1:
                hi, lo = split2(block.T)
                g_hi[ROWS * j:ROWS * (j + 1), ROWS * i:ROWS * (i + 1)] = hi
                g_lo[ROWS * j:ROWS * (j + 1), ROWS * i:ROWS * (i + 1)] = lo
    q_ref[...] = start_ref[...]

    def step(_, carry):
        image = dot3(q_ref[...], g_hi[...], g_lo[...])
        i_hi, i_lo = split2(image)
        both = dot_nt(jnp.concatenate([i_hi, i_lo], axis=0), i_hi)
        inner = both[:RANK] + (both[RANK:] + dot_nt(i_hi, i_lo))
        inverse_factor(inner, w_ref)
        q_ref[...] = dot3(w_ref[...], i_hi, i_lo)
        return carry

    lax.fori_loop(0, ITERS, step, 0)
    q = q_ref[...]
    d_hi, d_lo = split2(d_ref[...])
    core = dot3(q, d_hi, d_lo)
    mine_t = q_ref[:, pl.ds(pl.multiple_of(g * ROWS, ROWS), ROWS)]
    basis_ref[...] = mine_t
    mine = mine_t.T
    c_hi, c_lo = split2(core)
    out_ref[...] = dot3(mine, c_hi, c_lo)


def iterate(gathered, sums, start_t):
    cols = gathered.shape[1]
    return pl.pallas_call(
        iterate_kernel,
        out_shape=(jax.ShapeDtypeStruct((RANK, ROWS), f32), jax.ShapeDtypeStruct((ROWS, cols), f32)),
        in_specs=[pl.BlockSpec(memory_space=pltpu.VMEM)] * 3,
        out_specs=(pl.BlockSpec(memory_space=pltpu.VMEM),) * 2,
        scratch_shapes=[
            pltpu.VMEM((N, N), bf16), pltpu.VMEM((N, N), bf16),
            pltpu.VMEM((RANK, N), f32), pltpu.VMEM((RANK, RANK), f32)],
        compiler_params=pltpu.CompilerParams(vmem_limit_bytes=48 * 2**20),
    )(gathered, sums, start_t)


def body(snapshot, start):
    all_cells = snapshot.shape[1] * lax.axis_size("yz")
    gathered, sums = gather_and_gram(snapshot, all_cells)
    basis_t, projected = iterate(gathered.reshape(N, snapshot.shape[1]), sums, start.T)
    return basis_t.T, projected


def solution(mesh):
    in_specs = (P("gx", "yz"), P())
    out_specs = (P("gx", None), P("gx", "yz"))
    return jax.shard_map(body, mesh=mesh, in_specs=in_specs, out_specs=out_specs, check_vma=False)
```

time: 994 us -> 151 us (0.15)
  waiting for transfers between devices: 723 us -> 0 us
  other arithmetic: 195 us -> 0 us
  Pallas kernels: 0 us -> 145 us
  matrix products: 50.5 us -> 0 us
  between operations: 19.8 us -> 0.65 us
    psum x1 -> x0, waiting for transfers between devices: 566 us -> none  [body(): gram_block = lax.psum(gram_part, 'yz')]
    another operation x46 -> x0, other arithmetic: 194 us -> none  [the longest x28 115 us: body(): lower = jnp.linalg.cholesky(inner)]
    all_gather x2 -> x0, waiting for transfers between devices: 157 us -> none  [the longest x1 95.3 us: body(): gram = lax.all_gather(gram_block, 'gx', axis=0, tiled=True)]
    pallas_call x0 -> x2, Pallas kernels: none -> 145 us  [the longest x1 96.9 us: gather_and_gram(): pl.pallas_call(functools.partial(gram_kernel, all_cells), out_shape=(jax....]
    dot_general x11 -> x0, matrix products: 43.1 us -> none  [the longest x4 26 us: body(): image = jnp.dot(gram, basis_full, precision=highest)]
  transfers between devices with their start and end apart: 3 -> 0, of which waited for: 3 -> 0; matrix products, arithmetic and copies ran while one was open for 0% -> 0% of each run, Pallas kernels for 0% -> 0%
where the time goes in v1:
time: 151 us; the launch traced here: 150 us
  Pallas kernels  145 us (96%)
  local copies, waits for them, and re-layouts  4.1 us (3%)
    pallas_call x1, Pallas kernels, gather_and_gram(): pl.pallas_call(functools.partial(gram_kernel, all_cells), out_shape=(jax....  96.9 us
    pallas_call x1, Pallas kernels, iterate(): pl.pallas_call(iterate_kernel, out_shape=(jax.ShapeDtypeStruct((RANK, ROW...  48.6 us
    unnamed x6, local copies, waits for them, and re-layouts  4.1 us

profile of v1, /device:TPU:1, one launch (start us, length us, event | category | flops | bytes accessed | tf_op | source)
XLA Modules:
  0.0 150.2 jit_solution(979247766700153746)
XLA Ops:
  0.6 0.0 copy-start.2
  0.6 1.0 copy-done.2
  1.7 96.9 %shard_map.41 = (f32[8,128,1024]{2,1,0:T(8,128)S(1)}, f32[2,4,4,192,128]{4,3,2,1,0:T(8,128)S(1)}) custom-call(f32[128,1024]{1,0:T(8,128)S(1)} %copy-done.2), custom_call_target="tpu_custom_call" | custom-call | tf_op jit(solution)/shard_map/pallas_call | solution.py:192
  98.6 0.0 copy-start
  98.6 1.9 %copy-done = f32[8,128,1024]{2,1,0:T(8,128)} copy-done((f32[8,128,1024]{2,1,0:T(8,128)}, f32[8,128,1024]{2,1,0:T(8,128)S(1)}, u32[]{:S(2)}) %copy-start) | copy-done | bytes 4194328
  100.5 0.0 copy-start.1
  100.5 1.1 copy-done.1
  101.6 48.6 %shard_map.42 = (f32[192,128]{1,0:T(8,128)}, f32[128,1024]{1,0:T(8,128)}) custom-call(f32[1024,1024]{1,0:T(8,128)} %bitcast.3, f32[2,4,4,192,128]{4,3,2,1,0:T(8,128)S(1)} %get-tuple-element.7.f_ref, f32[192,1024]{1,0:T(8,128)S(1)} %bitcast.4), custom_call_target="tpu_custom_call" | custom-call | tf_op jit(solution)/shard_map/pallas_call | solution.py:313
Async XLA Ops:
  0.6 1.0 copy-start.2
  98.6 1.9 %copy-start = (f32[8,128,1024]{2,1,0:T(8,128)}, f32[8,128,1024]{2,1,0:T(8,128)S(1)}, u32[]{:S(2)}) copy-start(f32[8,128,1024]{2,1,0:T(8,128)S(1)} %get-tuple-element.6) | copy-start | bytes 12582916
  100.5 1.1 copy-start.1

commit v2 on v0

v2 whole, which is shorter than its diff:
```python
import functools
import jax
import jax.numpy as jnp
from jax import lax
from jax.experimental import pallas as pl
from jax.experimental.pallas import tpu as pltpu
from jax.sharding import PartitionSpec as P

ITERS = 4
G, NYH, NZ, NX, NYL, NY = 8, 4, 8, 4, 2, 8
ROWS = 128
XROWS = 176
ZROWS = 24
PAD = NZ * ZROWS
N = 1024
RANK = 192
PANEL = 32
f32, bf16 = jnp.float32, jnp.bfloat16
MESH = pl.DeviceIdType.MESH


def split2(a):
    hi = a.astype(jnp.bfloat16)
    lo = (a - hi.astype(jnp.float32)).astype(jnp.bfloat16)
    return hi, lo


def dot_nt(a, b):
    return lax.dot_general(a, b, (((1,), (1,)), ((), ())), preferred_element_type=jnp.float32)


def gram_kernel(cells, s_ref, hi_ref, lo_ref, f_ref, d_ref, parts, xin, xsum, zin, ysum, send, recv, local):
    g = lax.axis_index("gx")
    q = lax.axis_index("yz")
    yh, core = g // 2, g % 2
    z, x, yl = q // (NX * NYL), (q // NYL) % NX, q % NYL
    y = yh * NYL + yl

    def gx_at(yh2, core2):
        return (yh2 % NYH) * 2 + core2

    def yz_at(z2, x2, yl2):
        return ((z2 % NZ) * NX + x2 % NX) * NYL + yl2

    def y_peer(y2):
        return (gx_at((y2 % NY) // NYL, core), yz_at(z, x, y2 % NYL))

    def x_peer(k):
        return (g, yz_at(z, x + k, yl))

    def z_peer(k):
        return (g, yz_at(z + k, x, yl))

    pair = (gx_at(yh, 1 - core), q)
    right, left = (gx_at(yh + 1, core), q), (gx_at(yh + 3, core), q)
    peers = [pair] + [y_peer(y + k) for k in range(1, NY)]
    peers += [x_peer(k) for k in range(1, NX)] + [z_peer(k) for k in range(1, NZ)]

    barrier = pltpu.get_barrier_semaphore()
    for peer in peers:
        pl.semaphore_signal(barrier, inc=1, device_id=peer, device_id_type=MESH)
    mine = pltpu.make_async_copy(s_ref, d_ref.at[g], local)
    mine.start()
    pl.semaphore_wait(barrier, len(peers))

    sent = []
    count = [0]

    def slot(n=1):
        count[0] += n
        return count[0] - n

    def copy(src, dst, index, target):
        return pltpu.make_async_remote_copy(
            src_ref=src, dst_ref=dst, send_sem=send.at[index], recv_sem=recv.at[index],
            device_id=target, device_id_type=MESH)

    def push(ref, index, target, src=None):
        op = copy(ref if src is None else src, ref, index, target)
        op.start()
        sent.append(op)

    def arrived(ref, index):
        copy(ref, ref, index, pair).wait_recv()

    cols = s_ref.shape[1]
    half = cols // 2
    my_half = yh // 2

    def part(block, first, rows, which):
        return d_ref.at[block, pl.ds(first, rows), pl.ds(pl.multiple_of(which * half, half), half)]

    def here(block, which):
        return part(block, 0, ROWS, which)

    g_right, g_left, g_opp = right[0], left[0], gx_at(yh + 2, core)
    p_right, p_left, p_opp = (gx_at(yh + k, 1 - core) for k in (1, 3, 2))
    p_own = pair[0]
    s_pair, s_up, s_down, s_relay = slot(), slot(2), slot(2), slot(2)
    s_up2, s_relay2 = slot(), slot()
    f_right, f_opp, f_opp2, f_left, f_left2 = slot(2), slot(), slot(), slot(), slot()
    halfrows = ROWS // 2
    far = 1 - my_half

    def own(first, rows, which):
        return s_ref.at[pl.ds(first, rows), pl.ds(pl.multiple_of(which * half, half), half)]

    for c in range(2):
        push(part(g, halfrows * c, halfrows, far), s_up + c, right, own(halfrows * c, halfrows, far))
        push(here(g, c), s_down + c, left, own(0, ROWS, c))
    push(d_ref.at[g], s_pair, pair, s_ref)

    def split_into(block, which=None):
        if which is None:
            hi_ref[block], lo_ref[block] = split2(d_ref[block])
        else:
            lanes = pl.ds(pl.multiple_of(which * half, half), half)
            hi_ref[block, :, lanes], lo_ref[block, :, lanes] = split2(d_ref[block, :, lanes])

    def product(a, first, rows, b, which=None):
        lanes = slice(None) if which is None else pl.ds(pl.multiple_of(which * half, half), half)
        a_hi, a_lo = hi_ref[a, pl.ds(first, rows), lanes], lo_ref[a, pl.ds(first, rows), lanes]
        b_hi, b_lo = hi_ref[b, :, lanes], lo_ref[b, :, lanes]
        both = dot_nt(jnp.concatenate([a_hi, a_lo], axis=0), b_hi)
        return (both[:rows] + (both[rows:] + dot_nt(a_hi, b_lo))) * (1.0 / cells)

    def put(position, block):
        for k in range(NX):
            parts[k, pl.ds(pl.multiple_of(32 * position, 32), 32), :] = block[32 * k:32 * k + 32]

    mine.wait()
    split_into(g)
    put(0, product(g, 0, ROWS, g))
    arrived(d_ref.at[p_own], s_pair)
    split_into(p_own)
    block = product(gx_at(yh, 0), pl.multiple_of(halfrows * core, halfrows), halfrows, gx_at(yh, 1))
    for k in range(NX):
        parts[k, pl.ds(160, 16), :] = block[16 * k:16 * k + 16]
    for c in range(2):
        arrived(part(g_left, halfrows * c, halfrows, 1 - (yh + 3) % NYH // 2), s_up + c)
        push(part(g_left, halfrows * c, halfrows, 1 - (yh + 3) % NYH // 2), s_relay + c, right)
    for c in range(2):
        arrived(here(g_right, c), s_down + c)
        push(here(g_right, c), f_right + c, pair)
    for c in range(2):
        arrived(part(g_opp, halfrows * c, halfrows, my_half), s_relay + c)
    push(here(g_opp, my_half), f_opp, pair)
    push(here(g, my_half), s_up2, right)
    push(here(g_right, 1 - (yh + 3) % NYH // 2), s_relay2, left)
    push(here(g_left, 1 - (yh + 3) % NYH // 2), f_left, pair)
    split_into(g_right)
    put(1 + core, product(g, 0, ROWS, g_right))
    split_into(g_opp, my_half)
    put(3 + core, product(g, 0, ROWS, g_opp, my_half))
    for c in range(2):
        arrived(here(p_right, c), f_right + c)
    split_into(p_right)
    put(2 - core, product(g, 0, ROWS, p_right))
    arrived(here(p_opp, my_half), f_opp)
    split_into(p_opp, my_half)
    put(4 - core, product(g, 0, ROWS, p_opp, my_half))

    s_x = slot(NX)
    for k in range(1, NX):
        push(xin.at[k - 1], s_x + k, x_peer(k), parts.at[(x + k) % NX])
    xsum[pl.ds(XROWS, PAD - XROWS), :] = jnp.zeros((PAD - XROWS, 128), f32)
    total = parts[x]
    for k in range(1, NX):
        arrived(xin.at[k - 1], s_x + k)
        total += xin[k - 1]
    xsum[pl.ds(0, XROWS), :] = total

    def z_rows(z2):
        return pl.ds(pl.multiple_of(z2 % NZ * ZROWS, 8), ZROWS)

    s_z = slot(NZ)
    for k in range(1, NZ):
        push(zin.at[k - 1], s_z + k, z_peer(k), xsum.at[z_rows(z + k), :])
    total = xsum[z_rows(z), :]
    for k in range(1, NZ):
        arrived(zin.at[k - 1], s_z + k)
        total += zin[k - 1]
    ysum[y] = total
    s_y = slot(NY)
    for k in range(1, NY):
        push(ysum.at[y], s_y + k, y_peer(y + k))
    for k in range(1, NY):
        arrived(ysum.at[(y + k) % NY], s_y + (NY - k))
    for k in range(NYH):
        f_ref[core, x, z, k] = ysum[2 * k] + ysum[2 * k + 1]

    def slab(core2, kx, i):
        kz = (i % 2) * ((i + 1) // 2) + (1 - i % 2) * ((NZ - i // 2) % NZ)
        return f_ref.at[core2, (x + NX - kx) % NX, (z + NZ - kz) % NZ], kz

    s_az, s_right, s_left, s_far, s_ap = slot(NZ), slot(NZ), slot(NZ), slot(NZ), slot(NX * NZ)
    mine_f = f_ref.at[core, x, z]
    for i in range(1, NZ):
        kz = (i + 1) // 2 if i % 2 else NZ - i // 2
        push(mine_f, s_az + kz, z_peer(kz))

    def from_z(i, carry):
        ref, kz = slab(core, 0, i)

        @pl.when(i > 0)
        def _():
            arrived(ref, s_az + kz)

        copy(ref, ref, s_right + i, x_peer(1)).start()
        copy(ref, ref, s_left + i, x_peer(3)).start()
        copy(ref, ref, s_ap + i, pair).start()
        return carry

    lax.fori_loop(0, NZ, from_z, 0)

    def from_x(j, carry):
        for i, onward in ((2 * j, 1), (2 * j + 1, 3)):
            ref, _ = slab(core, 1, i)
            arrived(ref, s_right + i)
            if onward == 1:
                copy(ref, ref, s_far + i, x_peer(1)).start()
            copy(ref, ref, s_ap + NZ + i, pair).start()
            ref, _ = slab(core, 3, i)
            arrived(ref, s_left + i)
            if onward == 3:
                copy(ref, ref, s_far + i, x_peer(3)).start()
            copy(ref, ref, s_ap + 3 * NZ + i, pair).start()
        return carry

    lax.fori_loop(0, NZ // 2, from_x, 0)

    def from_far(i, carry):
        ref, _ = slab(core, 2, i)
        arrived(ref, s_far + i)
        copy(ref, ref, s_ap + 2 * NZ + i, pair).start()
        return carry

    lax.fori_loop(0, NZ, from_far, 0)

    left_half = (yh + 3) % NYH // 2
    arrived(here(g_left, left_half), s_up2)
    push(here(g_left, left_half), f_left2, pair)
    arrived(here(g_opp, far), s_relay2)
    push(here(g_opp, far), f_opp2, pair)
    split_into(g_left)
    split_into(g_opp, far)
    arrived(here(p_left, 1 - left_half), f_left)
    arrived(here(p_left, left_half), f_left2)
    split_into(p_left)
    arrived(here(p_opp, far), f_opp2)
    split_into(p_opp, far)

    def finish(i, carry):
        ref, _ = slab(core, 0, i)
        copy(ref, ref, s_right + i, x_peer(1)).wait_send()
        copy(ref, ref, s_left + i, x_peer(3)).wait_send()
        copy(ref, ref, s_far + i, x_peer(1)).wait_send()
        for kx in range(NX):
            ref, _ = slab(1 - core, kx, i)
            arrived(ref, s_ap + kx * NZ + i)
            copy(ref, ref, s_ap + kx * NZ + i, pair).wait_send()
        return carry

    lax.fori_loop(0, NZ, finish, 0)
    for op in sent:
        op.wait_send()


SLOTS = 1 + 2 + 2 + 2 + 2 + 6 + NX + NZ + NY + 4 * NZ + NX * NZ


def gather_and_gram(snapshot, all_cells):
    cols = snapshot.shape[1]
    vmem = pl.BlockSpec(memory_space=pltpu.VMEM)
    return pl.pallas_call(
        functools.partial(gram_kernel, all_cells),
        out_shape=(jax.ShapeDtypeStruct((G, ROWS, cols), bf16),
                   jax.ShapeDtypeStruct((G, ROWS, cols), bf16),
                   jax.ShapeDtypeStruct((2, NX, NZ, NYH, ZROWS, 128), f32)),
        in_specs=[vmem],
        out_specs=(vmem, vmem, vmem),
        scratch_shapes=[
            pltpu.VMEM((G, ROWS, cols), f32),
            pltpu.VMEM((NX, XROWS, 128), f32),
            pltpu.VMEM((NX - 1, XROWS, 128), f32),
            pltpu.VMEM((PAD, 128), f32),
            pltpu.VMEM((NZ - 1, ZROWS, 128), f32),
            pltpu.VMEM((NY, ZROWS, 128), f32),
            pltpu.SemaphoreType.DMA((SLOTS,)),
            pltpu.SemaphoreType.DMA((SLOTS,)),
            pltpu.SemaphoreType.DMA,
        ],
        compiler_params=pltpu.CompilerParams(
            collective_id=0, has_side_effects=True, vmem_limit_bytes=28 * 2**20),
    )(snapshot)


def dot(a, b):
    return lax.dot_general(a, b, (((1,), (0,)), ((), ())), preferred_element_type=f32)


def dot3(a, b_hi, b_lo, nt=False):
    d = dot_nt if nt else dot
    m = a.shape[0]
    a_hi, a_lo = split2(a)
    both = d(jnp.concatenate([a_hi, a_lo], axis=0), b_hi)
    return both[:m] + (both[m:] + d(a_hi, b_lo))


def reciprocal(x):
    r = pl.reciprocal(x, approx=True)
    return r * (2.0 - x * r)


def inverse_factor(m, w_ref):
    n = RANK
    lane = lax.broadcasted_iota(jnp.int32, (8, 128), 1)
    row = lax.broadcasted_iota(jnp.int32, (8, 128), 0)
    js = range(8)
    full = lambda v: jnp.broadcast_to(v, (8, 128))

    def stack(rows):
        t = rows[0]
        for j in js[1:]:
            t = jnp.where(row == j, rows[j], t)
        return t

    rest = jnp.concatenate([m, jnp.zeros((n, 256 - n), f32)], axis=1)
    for p0 in range(0, n, PANEL):
        tiles = [[rest[8 * i:8 * i + 8, 128 * h:128 * h + 128] for h in range(2)] for i in range(PANEL // 8)]
        below = rest[PANEL:]
        ct = p0 // 128
        for gi in range(PANEL // 8):
            c0 = p0 + 8 * gi
            cl = c0 - 128 * ct
            here = (lane >= cl) & (lane < cl + 8)
            t = tiles[gi]
            piv = [[None] * 8 for _ in js]
            for j in js:
                col = full(t[ct][:, cl + j:cl + j + 1])
                for i in range(j + 1):
                    piv[i][j] = full(col[i:i + 1])
            r = [[full(t[h][j:j + 1]) for h in range(2)] for j in js]
            for j in js:
                r[j][ct] = jnp.where(here, jnp.where(lane == cl + j, 1.0, 0.0), r[j][ct])
            inv = [None] * 8
            for j in js:
                inv[j] = reciprocal(piv[j][j])
                for i in range(j + 1, 8):
                    l = piv[j][i] * inv[j]
                    for k in range(i, 8):
                        piv[i][k] = piv[i][k] - l * piv[j][k]
                    for h in range(2):
                        r[i][h] = r[i][h] - l * r[j][h]
            for h in range(2):
                w = stack([r[j][h] * lax.rsqrt(piv[j][j]) for j in js])
                w_ref[c0:c0 + 8, 128 * h:128 * h + 128] = jnp.where(lane + 128 * h <= row + c0, w, 0.0)
            z = [None] * 8
            for j in reversed(js):
                z[j] = []
                for h in range(2):
                    v = r[j][h]
                    for i in range(7, j, -1):
                        v = v - piv[j][i] * z[i][h]
                    z[j].append(v * inv[j])
            for i in range(PANEL // 8):
                if i == gi:
                    continue
                cols = [full(tiles[i][ct][:, cl + j:cl + j + 1]) for j in js]
                old = tiles[i]
                tiles[i] = []
                for h in range(2):
                    v = jnp.where(here, 0.0, old[h]) if h == ct else old[h]
                    even = sum(cols[j] * z[j][h] for j in js[0::2])
                    odd = sum(cols[j] * z[j][h] for j in js[1::2])
                    tiles[i].append(v - (even + odd))
            tiles[gi] = [stack([z[j][h] for j in js]) for h in range(2)]
        if p0 + PANEL < n:
            a = jnp.concatenate([jnp.concatenate(t, axis=1) for t in tiles], axis=0)
            parts = [a]
            if p0 > 128 * ct:
                parts = [jnp.zeros((p0 - 128 * ct, 256), f32)] + parts
            after = 128 * ct + 128 - p0 - PANEL
            if after:
                parts = parts + [jnp.zeros((after, 256), f32)]
            z_hi, z_lo = split2(jnp.concatenate(parts, axis=0))
            lanes = lax.broadcasted_iota(jnp.int32, (1, 256), 1)
            in_panel = (lanes >= p0) & (lanes < p0 + PANEL)
            rest = jnp.where(in_panel, 0.0, below) - dot3(below[:, 128 * ct:128 * ct + 128], z_hi, z_lo)


def iterate_kernel(hi_ref, lo_ref, f_ref, start_ref, basis_ref, out_ref, g_hi, g_lo, i_ref, w_ref):
    g = lax.axis_index("gx")

    def store(i, j, block):
        hi, lo = split2(block)
        g_hi[ROWS * i:ROWS * (i + 1), ROWS * j:ROWS * (j + 1)] = hi
        g_lo[ROWS * i:ROWS * (i + 1), ROWS * j:ROWS * (j + 1)] = lo

    def rows(i, first, count):
        own = [f_ref[i % 2, k, :, i // 2].reshape(PAD, 128)[first:first + count] for k in range(NX)]
        return jnp.concatenate(own, axis=0)

    for yh in range(NYH):
        a, b = 2 * yh, 2 * yh + 1
        pair = jnp.concatenate([rows(a, 160, 16), rows(b, 160, 16)], axis=0)
        store(a, b, pair)
        store(b, a, pair.T)
        for i in (a, b):
            store(i, i, rows(i, 0, 32))
            for c in range(2):
                j = 2 * ((yh + 1) % NYH) + c
                block = rows(i, 32 * (1 + c), 32)
                store(i, j, block)
                store(j, i, block.T)
                j = 2 * ((yh + 2) % NYH) + c
                if yh < 2:
                    block = rows(i, 32 * (3 + c), 32) + rows(j, 32 * (3 + i % 2), 32).T
                    store(i, j, block)
                    store(j, i, block.T)
    i_ref[...] = dot3(start_ref[...], g_hi[...], g_lo[...])

    def factor(i_hi, i_lo):
        both = dot_nt(jnp.concatenate([i_hi, i_lo], axis=0), i_hi)
        inverse_factor(both[:RANK] + (both[RANK:] + dot_nt(i_hi, i_lo)), w_ref)

    def times(i_hi, i_lo, b_hi, b_lo):
        both = dot(jnp.concatenate([i_hi, i_lo], axis=0), b_hi)
        return both[:RANK] + (both[RANK:] + dot(i_hi, b_lo))

    def step(_, carry):
        i_hi, i_lo = split2(i_ref[...])
        after = times(i_hi, i_lo, g_hi[...], g_lo[...])
        factor(i_hi, i_lo)
        i_ref[...] = dot3(w_ref[:, :RANK], *split2(after))
        return carry

    lax.fori_loop(0, ITERS - 1, step, 0)
    i_hi, i_lo = split2(i_ref[...])
    after = times(i_hi, i_lo, hi_ref[...], lo_ref[...])
    factor(i_hi, i_lo)
    w = w_ref[:, :RANK]
    core = dot3(w, *split2(after))
    mine_t = dot3(w, *split2(i_ref[:, pl.ds(pl.multiple_of(g * ROWS, ROWS), ROWS)]))
    basis_ref[...] = mine_t
    out_ref[...] = dot3(mine_t.T, *split2(core))


def iterate(d_hi, d_lo, sums, start_t):
    cols = d_hi.shape[1]
    vmem = pl.BlockSpec(memory_space=pltpu.VMEM)
    return pl.pallas_call(
        iterate_kernel,
        out_shape=(jax.ShapeDtypeStruct((RANK, ROWS), f32), jax.ShapeDtypeStruct((ROWS, cols), f32)),
        in_specs=[vmem] * 4,
        out_specs=(vmem, vmem),
        scratch_shapes=[
            pltpu.VMEM((N, N), bf16), pltpu.VMEM((N, N), bf16),
            pltpu.VMEM((RANK, N), f32), pltpu.VMEM((RANK, 256), f32)],
        compiler_params=pltpu.CompilerParams(vmem_limit_bytes=28 * 2**20),
    )(d_hi, d_lo, sums, start_t)


def body(snapshot, start):
    all_cells = snapshot.shape[1] * lax.axis_size("yz")
    d_hi, d_lo, sums = gather_and_gram(snapshot, all_cells)
    shape = (N, snapshot.shape[1])
    basis_t, projected = iterate(d_hi.reshape(shape), d_lo.reshape(shape), sums, start.T)
    return basis_t.T, projected


def solution(mesh):
    in_specs = (P("gx", "yz"), P())
    out_specs = (P("gx", None), P("gx", "yz"))
    return jax.shard_map(body, mesh=mesh, in_specs=in_specs, out_specs=out_specs, check_vma=False)
```

time: 994 us -> 128 us (0.13)
  waiting for transfers between devices: 723 us -> 0 us
  other arithmetic: 195 us -> 0 us
  Pallas kernels: 0 us -> 125 us
  matrix products: 50.5 us -> 0 us
  between operations: 19.8 us -> 0.65 us
    psum x1 -> x0, waiting for transfers between devices: 566 us -> none  [body(): gram_block = lax.psum(gram_part, 'yz')]
    another operation x46 -> x0, other arithmetic: 194 us -> none  [the longest x28 115 us: body(): lower = jnp.linalg.cholesky(inner)]
    all_gather x2 -> x0, waiting for transfers between devices: 157 us -> none  [the longest x1 95.3 us: body(): gram = lax.all_gather(gram_block, 'gx', axis=0, tiled=True)]
    pallas_call x0 -> x2, Pallas kernels: none -> 125 us  [the longest x1 83.2 us: gather_and_gram(): pl.pallas_call(functools.partial(gram_kernel, all_cells), out_shape=(jax....]
    dot_general x11 -> x0, matrix products: 43.1 us -> none  [the longest x4 26 us: body(): image = jnp.dot(gram, basis_full, precision=highest)]
  transfers between devices with their start and end apart: 3 -> 0, of which waited for: 3 -> 0; matrix products, arithmetic and copies ran while one was open for 0% -> 0% of each run, Pallas kernels for 0% -> 0%
where the time goes in v2:
time: 128 us
  Pallas kernels  125 us (98%)
  local copies, waits for them, and re-layouts  2.16 us (2%)
    pallas_call x1, Pallas kernels, gather_and_gram(): pl.pallas_call(functools.partial(gram_kernel, all_cells), out_shape=(jax....  83.2 us
    pallas_call x1, Pallas kernels, iterate(): pl.pallas_call(iterate_kernel, out_shape=(jax.ShapeDtypeStruct((RANK, ROW...  42 us

profile of v2, /device:TPU:1, one launch (start us, length us, event | category | flops | bytes accessed | tf_op | source)
XLA Modules:
  0.0 128.0 jit_solution(7957934938755047839)
XLA Ops:
  0.6 0.0 copy-start.1
  0.6 1.0 copy-done.1
  1.7 83.2 %shard_map.41 = (bf16[8,128,1024]{2,1,0:T(8,128)(2,1)S(1)}, bf16[8,128,1024]{2,1,0:T(8,128)(2,1)S(1)}, f32[2,4,8,4,24,128]{5,4,3,2,1,0:T(8,128)S(1)}) custom-call(f32[128,1024]{1,0:T(8,128)S(1)} %copy-done.1), custom_call_target="tpu_custom_call" | custom-call | tf_op jit(solution)/shard_map/pallas_call | solution.py:275
  84.9 0.0 copy-start
  84.9 1.1 copy-done
  86.0 42.0 %shard_map.42 = (f32[192,128]{1,0:T(8,128)}, f32[128,1024]{1,0:T(8,128)}) custom-call(bf16[1024,1024]{1,0:T(8,128)(2,1)S(1)} %bitcast.4, bf16[1024,1024]{1,0:T(8,128)(2,1)S(1)} %bitcast.5, f32[2,4,8,4,24,128]{5,4,3,2,1,0:T(8,128)S(1)} %get-tuple-element.9.f_ref, f32[192,1024]{1,0:T(8,128)S(1)} %bitcast.6), custom_call_target="tpu_custom_call" | custom-call | tf_op jit(solution)/shard_map/pallas_call | solution.py:452
Async XLA Ops:
  0.6 1.0 copy-start.1
  84.9 1.1 copy-start

commit v3 on v2

--- a/solution.py
+++ b/solution.py
@@ -9,9 +9,7 @@
 ITERS = 4
 G, NYH, NZ, NX, NYL, NY = 8, 4, 8, 4, 2, 8
 ROWS = 128
-XROWS = 176
-ZROWS = 24
-PAD = NZ * ZROWS
+KINDS = 4
 N = 1024
 RANK = 192
 PANEL = 32
@@ -83,190 +81,220 @@
     def arrived(ref, index):
         copy(ref, ref, index, pair).wait_recv()
 
-    cols = s_ref.shape[1]
-    half = cols // 2
-    my_half = yh // 2
-
-    def part(block, first, rows, which):
-        return d_ref.at[block, pl.ds(first, rows), pl.ds(pl.multiple_of(which * half, half), half)]
-
-    def here(block, which):
-        return part(block, 0, ROWS, which)
+    quarter = s_ref.shape[1] // 4
+    mine_q = yh // 2
+    far_q = 1 - mine_q
+    right_q = 1 - (yh + 1) % NYH // 2
+    left_q = 1 - (yh + 3) % NYH // 2
+
+    def lanes(first, n):
+        return pl.ds(pl.multiple_of(first * quarter, quarter), n * quarter)
+
+    def cells_of(block, first, n=1):
+        return d_ref.at[block, :, lanes(first, n)]
+
+    def own(first, n=1):
+        return s_ref.at[:, lanes(first, n)]
 
     g_right, g_left, g_opp = right[0], left[0], gx_at(yh + 2, core)
+    p_own = pair[0]
     p_right, p_left, p_opp = (gx_at(yh + k, 1 - core) for k in (1, 3, 2))
-    p_own = pair[0]
-    s_pair, s_up, s_down, s_relay = slot(), slot(2), slot(2), slot(2)
-    s_up2, s_relay2 = slot(), slot()
-    f_right, f_opp, f_opp2, f_left, f_left2 = slot(2), slot(), slot(), slot(), slot()
+    s_pair, s_down, s_up, s_relay = slot(), slot(2), slot(2), slot(2)
+    f_right, f_left, f_opp = slot(2), slot(2), slot(2)
+    push(cells_of(g, far_q), s_down, left, own(far_q))
+    push(cells_of(g, 2 + far_q), s_up, right, own(2 + far_q))
+    push(d_ref.at[g], s_pair, pair, s_ref)
+    push(cells_of(g, mine_q), s_down + 1, left, own(mine_q))
+    push(cells_of(g, 2 + mine_q), s_up + 1, right, own(2 + mine_q))
+
+    def split_into(block, first, n):
+        where = lanes(first, n)
+        hi_ref[block, :, where], lo_ref[block, :, where] = split2(d_ref[block, :, where])
+
+    def product(a, b, segments, first=0, rows=ROWS):
+        total = None
+        for begin, n in segments:
+            where = lanes(begin, n)
+            a_hi, a_lo = hi_ref[a, pl.ds(first, rows), where], lo_ref[a, pl.ds(first, rows), where]
+            b_hi, b_lo = hi_ref[b, :, where], lo_ref[b, :, where]
+            both = dot_nt(jnp.concatenate([a_hi, a_lo], axis=0), b_hi)
+            term = both[:rows] + (both[rows:] + dot_nt(a_hi, b_lo))
+            total = term if total is None else total + term
+        return total * (1.0 / cells)
+
+    def put(kind, position, block):
+        rows = block.shape[0] // NX
+        for k in range(NX):
+            parts[k, kind, position:position + rows // 8] = block[rows * k:rows * (k + 1)].reshape(rows // 8, 8, 128)
+
+    class Sums:
+        def __init__(self, lo, n):
+            self.kinds = pl.ds(lo, n)
+            self.x, self.z, self.y = slot(NX), slot(NZ), slot(NY)
+
+        def send_x(self):
+            for k in range(1, NX):
+                push(xin.at[k - 1, self.kinds], self.x + k, x_peer(k), parts.at[(x + k) % NX, self.kinds])
+
+        def send_z(self):
+            total = parts[x, self.kinds]
+            for k in range(1, NX):
+                arrived(xin.at[k - 1, self.kinds], self.x + k)
+                total += xin[k - 1, self.kinds]
+            xsum[self.kinds] = total
+            for k in range(1, NZ):
+                push(zin.at[k - 1, self.kinds], self.z + k, z_peer(k), xsum.at[self.kinds, (z + k) % NZ])
+
+        def send_y(self):
+            total = xsum[self.kinds, z]
+            for k in range(1, NZ):
+                arrived(zin.at[k - 1, self.kinds], self.z + k)
+                total += zin[k - 1, self.kinds]
+            ysum[y, self.kinds] = total
+            for k in range(1, NY):
+                push(ysum.at[y, self.kinds], self.y + k, y_peer(y + k))
+
+        def finish(self):
+            for k in range(1, NY):
+                arrived(ysum.at[(y + NY - k) % NY, self.kinds], self.y + k)
+
+    class Spread:
+        def __init__(self, lo, n):
+            self.tiles = pl.ds(lo, n)
+            self.z, self.x, self.pair = slot(NZ), slot(NX), slot(NX)
+
+        def part(self, core2, k):
+            return f_ref.at[core2, (x + NX - k) % NX, :, self.tiles]
+
+        def send_z(self):
+            for k in (1, 7, 2, 6, 3, 5, 4):
+                push(f_ref.at[core, x, z, self.tiles], self.z + k, z_peer(k))
+
+        def send_x(self):
+            for k in range(1, NZ):
+                arrived(f_ref.at[core, x, (z + NZ - k) % NZ, self.tiles], self.z + k)
+            for k in (2, 1, 3):
+                push(self.part(core, 0), self.x + k, x_peer(k))
+            push(self.part(core, 0), self.pair, pair)
+
+        def send_pair(self):
+            for k in (1, 3, 2):
+                arrived(self.part(core, k), self.x + k)
+                push(self.part(core, k), self.pair + k, pair)
+
+        def finish(self):
+            for k in range(NX):
+                arrived(self.part(1 - core, k), self.pair + k)
+
+    sum_own, sum_near, sum_opp = Sums(0, 1), Sums(1, 2), Sums(3, 1)
+    all_own, all_near, all_opp = Spread(0, NYH), Spread(NYH, NYH), Spread(2 * NYH, 2)
+
+    mine.wait()
+    split_into(g, 0, 4)
+    put(0, 0, product(g, g, [(0, 4)]))
+    arrived(d_ref.at[p_own], s_pair)
+    split_into(p_own, 0, 4)
     halfrows = ROWS // 2
-    far = 1 - my_half
-
-    def own(first, rows, which):
-        return s_ref.at[pl.ds(first, rows), pl.ds(pl.multiple_of(which * half, half), half)]
-
+    first = pl.multiple_of(halfrows * core, halfrows)
+    put(0, 4, product(gx_at(yh, 0), gx_at(yh, 1), [(0, 4)], first, halfrows))
+    for k in range(NX):
+        parts[k, 0, 6:8] = jnp.zeros((2, 8, 128), f32)
+    sum_own.send_x()
+
+    arrived(cells_of(g_right, right_q), s_down)
+    push(cells_of(g_right, right_q), s_relay, left)
+    push(cells_of(g_right, right_q), f_right, pair)
+    arrived(cells_of(g_left, 2 + left_q), s_up)
+    push(cells_of(g_left, 2 + left_q), s_relay + 1, right)
+    push(cells_of(g_left, 2 + left_q), f_left, pair)
+    sum_own.send_z()
+    arrived(cells_of(g_right, 1 - right_q), s_down + 1)
+    push(cells_of(g_right, 1 - right_q), f_right + 1, pair)
+    arrived(cells_of(g_left, 3 - left_q), s_up + 1)
+    push(cells_of(g_left, 3 - left_q), f_left + 1, pair)
+    sum_own.send_y()
+    split_into(g_right, 0, 2)
+    split_into(g_left, 2, 2)
+    arrived(cells_of(p_right, right_q), f_right)
+    arrived(cells_of(p_right, 1 - right_q), f_right + 1)
+    split_into(p_right, 0, 2)
     for c in range(2):
-        push(part(g, halfrows * c, halfrows, far), s_up + c, right, own(halfrows * c, halfrows, far))
-        push(here(g, c), s_down + c, left, own(0, ROWS, c))
-    push(d_ref.at[g], s_pair, pair, s_ref)
-
-    def split_into(block, which=None):
-        if which is None:
-            hi_ref[block], lo_ref[block] = split2(d_ref[block])
-        else:
-            lanes = pl.ds(pl.multiple_of(which * half, half), half)
-            hi_ref[block, :, lanes], lo_ref[block, :, lanes] = split2(d_ref[block, :, lanes])
-
-    def product(a, first, rows, b, which=None):
-        lanes = slice(None) if which is None else pl.ds(pl.multiple_of(which * half, half), half)
-        a_hi, a_lo = hi_ref[a, pl.ds(first, rows), lanes], lo_ref[a, pl.ds(first, rows), lanes]
-        b_hi, b_lo = hi_ref[b, :, lanes], lo_ref[b, :, lanes]
-        both = dot_nt(jnp.concatenate([a_hi, a_lo], axis=0), b_hi)
-        return (both[:rows] + (both[rows:] + dot_nt(a_hi, b_lo))) * (1.0 / cells)
-
-    def put(position, block):
-        for k in range(NX):
-            parts[k, pl.ds(pl.multiple_of(32 * position, 32), 32), :] = block[32 * k:32 * k + 32]
-
-    mine.wait()
-    split_into(g)
-    put(0, product(g, 0, ROWS, g))
-    arrived(d_ref.at[p_own], s_pair)
-    split_into(p_own)
-    block = product(gx_at(yh, 0), pl.multiple_of(halfrows * core, halfrows), halfrows, gx_at(yh, 1))
-    for k in range(NX):
-        parts[k, pl.ds(160, 16), :] = block[16 * k:16 * k + 16]
+        put(1, 4 * c, product(g, gx_at(yh + 1, c), [(0, 2)]))
+        put(2, 4 * c, product(g_left, gx_at(yh, c), [(2, 2)]))
+    sum_near.send_x()
+    sum_own.finish()
+    for k in range(NYH):
+        f_ref[core, x, z, k] = ysum[2 * k, 0] + ysum[2 * k + 1, 0]
+    all_own.send_z()
+
+    arrived(cells_of(g_opp, mine_q), s_relay)
+    push(cells_of(g_opp, mine_q), f_opp, pair)
+    arrived(cells_of(g_opp, 2 + mine_q), s_relay + 1)
+    push(cells_of(g_opp, 2 + mine_q), f_opp + 1, pair)
+    l_right, l_left, l_relay, l_pair = slot(), slot(), slot(2), slot(4)
+    push(cells_of(g_right, 1 - right_q), l_relay, left)
+    push(cells_of(g_left, 3 - left_q), l_relay + 1, right)
+    push(cells_of(g, 0, 2), l_right, right, own(0, 2))
+    push(cells_of(g, 2, 2), l_left, left, own(2, 2))
+    split_into(g_opp, mine_q, 1)
+    split_into(g_opp, 2 + mine_q, 1)
+    sum_near.send_z()
+    arrived(cells_of(p_opp, mine_q), f_opp)
+    split_into(p_opp, mine_q, 1)
+    arrived(cells_of(p_opp, 2 + mine_q), f_opp + 1)
+    split_into(p_opp, 2 + mine_q, 1)
     for c in range(2):
-        arrived(part(g_left, halfrows * c, halfrows, 1 - (yh + 3) % NYH // 2), s_up + c)
-        push(part(g_left, halfrows * c, halfrows, 1 - (yh + 3) % NYH // 2), s_relay + c, right)
-    for c in range(2):
-        arrived(here(g_right, c), s_down + c)
-        push(here(g_right, c), f_right + c, pair)
-    for c in range(2):
-        arrived(part(g_opp, halfrows * c, halfrows, my_half), s_relay + c)
-    push(here(g_opp, my_half), f_opp, pair)
-    push(here(g, my_half), s_up2, right)
-    push(here(g_right, 1 - (yh + 3) % NYH // 2), s_relay2, left)
-    push(here(g_left, 1 - (yh + 3) % NYH // 2), f_left, pair)
-    split_into(g_right)
-    put(1 + core, product(g, 0, ROWS, g_right))
-    split_into(g_opp, my_half)
-    put(3 + core, product(g, 0, ROWS, g_opp, my_half))
-    for c in range(2):
-        arrived(here(p_right, c), f_right + c)
-    split_into(p_right)
-    put(2 - core, product(g, 0, ROWS, p_right))
-    arrived(here(p_opp, my_half), f_opp)
-    split_into(p_opp, my_half)
-    put(4 - core, product(g, 0, ROWS, p_opp, my_half))
-
-    s_x = slot(NX)
-    for k in range(1, NX):
-        push(xin.at[k - 1], s_x + k, x_peer(k), parts.at[(x + k) % NX])
-    xsum[pl.ds(XROWS, PAD - XROWS), :] = jnp.zeros((PAD - XROWS, 128), f32)
-    total = parts[x]
-    for k in range(1, NX):
-        arrived(xin.at[k - 1], s_x + k)
-        total += xin[k - 1]
-    xsum[pl.ds(0, XROWS), :] = total
-
-    def z_rows(z2):
-        return pl.ds(pl.multiple_of(z2 % NZ * ZROWS, 8), ZROWS)
-
-    s_z = slot(NZ)
-    for k in range(1, NZ):
-        push(zin.at[k - 1], s_z + k, z_peer(k), xsum.at[z_rows(z + k), :])
-    total = xsum[z_rows(z), :]
-    for k in range(1, NZ):
-        arrived(zin.at[k - 1], s_z + k)
-        total += zin[k - 1]
-    ysum[y] = total
-    s_y = slot(NY)
-    for k in range(1, NY):
-        push(ysum.at[y], s_y + k, y_peer(y + k))
-    for k in range(1, NY):
-        arrived(ysum.at[(y + k) % NY], s_y + (NY - k))
+        put(3, 4 * c, product(gx_at(yh % 2, core), gx_at(yh % 2 + 2, c), [(mine_q, 1), (2 + mine_q, 1)]))
+    sum_opp.send_x()
+    all_own.send_x()
+    sum_near.send_y()
+    sum_opp.send_z()
+    sum_near.finish()
     for k in range(NYH):
-        f_ref[core, x, z, k] = ysum[2 * k] + ysum[2 * k + 1]
-
-    def slab(core2, kx, i):
-        kz = (i % 2) * ((i + 1) // 2) + (1 - i % 2) * ((NZ - i // 2) % NZ)
-        return f_ref.at[core2, (x + NX - kx) % NX, (z + NZ - kz) % NZ], kz
-
-    s_az, s_right, s_left, s_far, s_ap = slot(NZ), slot(NZ), slot(NZ), slot(NZ), slot(NX * NZ)
-    mine_f = f_ref.at[core, x, z]
-    for i in range(1, NZ):
-        kz = (i + 1) // 2 if i % 2 else NZ - i // 2
-        push(mine_f, s_az + kz, z_peer(kz))
-
-    def from_z(i, carry):
-        ref, kz = slab(core, 0, i)
-
-        @pl.when(i > 0)
-        def _():
-            arrived(ref, s_az + kz)
-
-        copy(ref, ref, s_right + i, x_peer(1)).start()
-        copy(ref, ref, s_left + i, x_peer(3)).start()
-        copy(ref, ref, s_ap + i, pair).start()
-        return carry
-
-    lax.fori_loop(0, NZ, from_z, 0)
-
-    def from_x(j, carry):
-        for i, onward in ((2 * j, 1), (2 * j + 1, 3)):
-            ref, _ = slab(core, 1, i)
-            arrived(ref, s_right + i)
-            if onward == 1:
-                copy(ref, ref, s_far + i, x_peer(1)).start()
-            copy(ref, ref, s_ap + NZ + i, pair).start()
-            ref, _ = slab(core, 3, i)
-            arrived(ref, s_left + i)
-            if onward == 3:
-                copy(ref, ref, s_far + i, x_peer(3)).start()
-            copy(ref, ref, s_ap + 3 * NZ + i, pair).start()
-        return carry
-
-    lax.fori_loop(0, NZ // 2, from_x, 0)
-
-    def from_far(i, carry):
-        ref, _ = slab(core, 2, i)
-        arrived(ref, s_far + i)
-        copy(ref, ref, s_ap + 2 * NZ + i, pair).start()
-        return carry
-
-    lax.fori_loop(0, NZ, from_far, 0)
-
-    left_half = (yh + 3) % NYH // 2
-    arrived(here(g_left, left_half), s_up2)
-    push(here(g_left, left_half), f_left2, pair)
-    arrived(here(g_opp, far), s_relay2)
-    push(here(g_opp, far), f_opp2, pair)
-    split_into(g_left)
-    split_into(g_opp, far)
-    arrived(here(p_left, 1 - left_half), f_left)
-    arrived(here(p_left, left_half), f_left2)
-    split_into(p_left)
-    arrived(here(p_opp, far), f_opp2)
-    split_into(p_opp, far)
-
-    def finish(i, carry):
-        ref, _ = slab(core, 0, i)
-        copy(ref, ref, s_right + i, x_peer(1)).wait_send()
-        copy(ref, ref, s_left + i, x_peer(3)).wait_send()
-        copy(ref, ref, s_far + i, x_peer(1)).wait_send()
-        for kx in range(NX):
-            ref, _ = slab(1 - core, kx, i)
-            arrived(ref, s_ap + kx * NZ + i)
-            copy(ref, ref, s_ap + kx * NZ + i, pair).wait_send()
-        return carry
-
-    lax.fori_loop(0, NZ, finish, 0)
+        after = (k + 1) % NYH
+        f_ref[core, x, z, NYH + k] = (ysum[2 * k, 1] + ysum[2 * k + 1, 1]) + (ysum[2 * after, 2] + ysum[2 * after + 1, 2])
+    all_near.send_z()
+    sum_opp.send_y()
+    all_own.send_pair()
+    sum_opp.finish()
+    for k in range(2):
+        f_ref[core, x, z, 2 * NYH + k] = (ysum[2 * k, 3] + ysum[2 * k + 1, 3]) + (ysum[2 * k + 4, 3] + ysum[2 * k + 5, 3])
+    all_opp.send_z()
+    all_near.send_x()
+    all_opp.send_x()
+    arrived(cells_of(g_opp, far_q), l_relay)
+    push(cells_of(g_opp, far_q), l_pair, pair)
+    arrived(cells_of(g_opp, 2 + far_q), l_relay + 1)
+    push(cells_of(g_opp, 2 + far_q), l_pair + 1, pair)
+    split_into(g_opp, far_q, 1)
+    split_into(g_opp, 2 + far_q, 1)
+    arrived(cells_of(p_left, 2 + left_q), f_left)
+    arrived(cells_of(p_left, 3 - left_q), f_left + 1)
+    split_into(p_left, 2, 2)
+    all_near.send_pair()
+    all_opp.send_pair()
+    arrived(cells_of(g_left, 0, 2), l_right)
+    push(cells_of(g_left, 0, 2), l_pair + 2, pair)
+    arrived(cells_of(g_right, 2, 2), l_left)
+    push(cells_of(g_right, 2, 2), l_pair + 3, pair)
+    split_into(g_left, 0, 2)
+    split_into(g_right, 2, 2)
+    arrived(cells_of(p_opp, far_q), l_pair)
+    split_into(p_opp, far_q, 1)
+    arrived(cells_of(p_opp, 2 + far_q), l_pair + 1)
+    split_into(p_opp, 2 + far_q, 1)
+    arrived(cells_of(p_left, 0, 2), l_pair + 2)
+    split_into(p_left, 0, 2)
+    arrived(cells_of(p_right, 2, 2), l_pair + 3)
+    split_into(p_right, 2, 2)
+    for group in (all_own, all_near, all_opp):
+        group.finish()
     for op in sent:
         op.wait_send()
 
 
-SLOTS = 1 + 2 + 2 + 2 + 2 + 6 + NX + NZ + NY + 4 * NZ + NX * NZ
+TILES = 2 * NYH + 2
+SLOTS = 13 + 8 + 3 * (NX + NZ + NY) + 3 * (NZ + 2 * NX)
 
 
 def gather_and_gram(snapshot, all_cells):
@@ -276,16 +304,16 @@
         functools.partial(gram_kernel, all_cells),
         out_shape=(jax.ShapeDtypeStruct((G, ROWS, cols), bf16),
                    jax.ShapeDtypeStruct((G, ROWS, cols), bf16),
-                   jax.ShapeDtypeStruct((2, NX, NZ, NYH, ZROWS, 128), f32)),
+                   jax.ShapeDtypeStruct((2, NX, NZ, TILES, 8, 128), f32)),
         in_specs=[vmem],
         out_specs=(vmem, vmem, vmem),
         scratch_shapes=[
             pltpu.VMEM((G, ROWS, cols), f32),
-            pltpu.VMEM((NX, XROWS, 128), f32),
-            pltpu.VMEM((NX - 1, XROWS, 128), f32),
-            pltpu.VMEM((PAD, 128), f32),
-            pltpu.VMEM((NZ - 1, ZROWS, 128), f32),
-            pltpu.VMEM((NY, ZROWS, 128), f32),
+            pltpu.VMEM((NX, KINDS, NZ, 8, 128), f32),
+            pltpu.VMEM((NX - 1, KINDS, NZ, 8, 128), f32),
+            pltpu.VMEM((KINDS, NZ, 8, 128), f32),
+            pltpu.VMEM((NZ - 1, KINDS, 8, 128), f32),
+            pltpu.VMEM((NY, KINDS, 8, 128), f32),
             pltpu.SemaphoreType.DMA((SLOTS,)),
             pltpu.SemaphoreType.DMA((SLOTS,)),
             pltpu.SemaphoreType.DMA,
@@ -392,32 +420,35 @@
 def iterate_kernel(hi_ref, lo_ref, f_ref, start_ref, basis_ref, out_ref, g_hi, g_lo, i_ref, w_ref):
     g = lax.axis_index("gx")
 
+
     def store(i, j, block):
         hi, lo = split2(block)
         g_hi[ROWS * i:ROWS * (i + 1), ROWS * j:ROWS * (j + 1)] = hi
         g_lo[ROWS * i:ROWS * (i + 1), ROWS * j:ROWS * (j + 1)] = lo
 
-    def rows(i, first, count):
-        own = [f_ref[i % 2, k, :, i // 2].reshape(PAD, 128)[first:first + count] for k in range(NX)]
+    def rows(core, tile, first, count):
+        own = [f_ref[core, k, :, tile].reshape(NZ * 8, 128)[first:first + count] for k in range(NX)]
         return jnp.concatenate(own, axis=0)
 
     for yh in range(NYH):
         a, b = 2 * yh, 2 * yh + 1
-        pair = jnp.concatenate([rows(a, 160, 16), rows(b, 160, 16)], axis=0)
+        pair = jnp.concatenate([rows(0, yh, 32, 16), rows(1, yh, 32, 16)], axis=0)
         store(a, b, pair)
         store(b, a, pair.T)
-        for i in (a, b):
-            store(i, i, rows(i, 0, 32))
+        for core in range(2):
+            i = 2 * yh + core
+            store(i, i, rows(core, yh, 0, 32))
             for c in range(2):
                 j = 2 * ((yh + 1) % NYH) + c
-                block = rows(i, 32 * (1 + c), 32)
+                block = rows(core, NYH + yh, 32 * c, 32)
                 store(i, j, block)
                 store(j, i, block.T)
-                j = 2 * ((yh + 2) % NYH) + c
                 if yh < 2:
-                    block = rows(i, 32 * (3 + c), 32) + rows(j, 32 * (3 + i % 2), 32).T
+                    j = 2 * (yh + 2) + c
+                    block = rows(core, 2 * NYH + yh, 32 * c, 32)
                     store(i, j, block)
                     store(j, i, block.T)
+
     i_ref[...] = dot3(start_ref[...], g_hi[...], g_lo[...])
 
     def factor(i_hi, i_lo):

time: 128 us -> 121 us (0.945)
  Pallas kernels: 125 us -> 118 us
    pallas_call x1, Pallas kernels: 83.2 us -> 76.6 us  [gather_and_gram(): pl.pallas_call(functools.partial(gram_kernel, all_cells), out_shape=(jax....]
where the time goes in v3:
time: 121 us
  Pallas kernels  118 us (98%)
  local copies, waits for them, and re-layouts  2.16 us (2%)
    pallas_call x1, Pallas kernels, gather_and_gram(): pl.pallas_call(functools.partial(gram_kernel, all_cells), out_shape=(jax....  76.6 us
    pallas_call x1, Pallas kernels, iterate(): pl.pallas_call(iterate_kernel, out_shape=(jax.ShapeDtypeStruct((RANK, ROW...  41.9 us

profile of v3, /device:TPU:1, one launch (start us, length us, event | category | flops | bytes accessed | tf_op | source)
XLA Modules:
  0.0 121.2 jit_solution(12677253905205419671)
XLA Ops:
  0.6 0.0 copy-start.1
  0.6 1.0 copy-done.1
  1.7 76.6 %shard_map.41 = (bf16[8,128,1024]{2,1,0:T(8,128)(2,1)S(1)}, bf16[8,128,1024]{2,1,0:T(8,128)(2,1)S(1)}, f32[2,4,8,10,8,128]{5,4,3,2,1,0:T(8,128)S(1)}) custom-call(f32[128,1024]{1,0:T(8,128)S(1)} %copy-done.1), custom_call_target="tpu_custom_call" | custom-call | tf_op jit(solution)/shard_map/pallas_call | solution.py:303
  78.2 0.0 copy-start
  78.3 1.1 copy-done
  79.4 41.9 %shard_map.42 = (f32[192,128]{1,0:T(8,128)}, f32[128,1024]{1,0:T(8,128)}) custom-call(bf16[1024,1024]{1,0:T(8,128)(2,1)S(1)} %bitcast.4, bf16[1024,1024]{1,0:T(8,128)(2,1)S(1)} %bitcast.5, f32[2,4,8,10,8,128]{5,4,3,2,1,0:T(8,128)S(1)} %get-tuple-element.9.f_ref, f32[192,1024]{1,0:T(8,128)S(1)} %bitcast.6), custom_call_target="tpu_custom_call" | custom-call | tf_op jit(solution)/shard_map/pallas_call | solution.py:483
Async XLA Ops:
  0.6 1.0 copy-start.1
  78.2 1.1 copy-start

commit v4 on v3

--- a/solution.py
+++ b/solution.py
@@ -10,6 +10,7 @@
 G, NYH, NZ, NX, NYL, NY = 8, 4, 8, 4, 2, 8
 ROWS = 128
 KINDS = 4
+RING_ORDER = (4, 3, 5, 2, 6, 1, 7)
 N = 1024
 RANK = 192
 PANEL = 32
@@ -125,7 +126,7 @@
     def put(kind, position, block):
         rows = block.shape[0] // NX
         for k in range(NX):
-            parts[k, kind, position:position + rows // 8] = block[rows * k:rows * (k + 1)].reshape(rows // 8, 8, 128)
+            parts[k, kind, pl.ds(position, rows // 8)] = block[rows * k:rows * (k + 1)].reshape(rows // 8, 8, 128)
 
     class Sums:
         def __init__(self, lo, n):
@@ -133,7 +134,7 @@
             self.x, self.z, self.y = slot(NX), slot(NZ), slot(NY)
 
         def send_x(self):
-            for k in range(1, NX):
+            for k in (2, 1, 3):
                 push(xin.at[k - 1, self.kinds], self.x + k, x_peer(k), parts.at[(x + k) % NX, self.kinds])
 
         def send_z(self):
@@ -142,7 +143,7 @@
                 arrived(xin.at[k - 1, self.kinds], self.x + k)
                 total += xin[k - 1, self.kinds]
             xsum[self.kinds] = total
-            for k in range(1, NZ):
+            for k in RING_ORDER:
                 push(zin.at[k - 1, self.kinds], self.z + k, z_peer(k), xsum.at[self.kinds, (z + k) % NZ])
 
         def send_y(self):
@@ -151,7 +152,7 @@
                 arrived(zin.at[k - 1, self.kinds], self.z + k)
                 total += zin[k - 1, self.kinds]
             ysum[y, self.kinds] = total
-            for k in range(1, NY):
+            for k in RING_ORDER:
                 push(ysum.at[y, self.kinds], self.y + k, y_peer(y + k))
 
         def finish(self):
@@ -167,7 +168,7 @@
             return f_ref.at[core2, (x + NX - k) % NX, :, self.tiles]
 
         def send_z(self):
-            for k in (1, 7, 2, 6, 3, 5, 4):
+            for k in RING_ORDER:
                 push(f_ref.at[core, x, z, self.tiles], self.z + k, z_peer(k))
 
         def send_x(self):
@@ -212,15 +213,21 @@
     push(cells_of(g_right, 1 - right_q), f_right + 1, pair)
     arrived(cells_of(g_left, 3 - left_q), s_up + 1)
     push(cells_of(g_left, 3 - left_q), f_left + 1, pair)
+    l_right, l_left, l_relay, l_pair = slot(), slot(), slot(2), slot(4)
+    push(cells_of(g_right, 1 - right_q), l_relay, left)
+    push(cells_of(g_left, 3 - left_q), l_relay + 1, right)
+    push(cells_of(g, 0, 2), l_right, right, own(0, 2))
+    push(cells_of(g, 2, 2), l_left, left, own(2, 2))
     sum_own.send_y()
     split_into(g_right, 0, 2)
     split_into(g_left, 2, 2)
+    for c in range(2):
+        put(2, 4 * c, product(g_left, gx_at(yh, c), [(2, 2)]))
+    put(1, 4 * core, product(g, g_right, [(0, 2)]))
     arrived(cells_of(p_right, right_q), f_right)
     arrived(cells_of(p_right, 1 - right_q), f_right + 1)
     split_into(p_right, 0, 2)
-    for c in range(2):
-        put(1, 4 * c, product(g, gx_at(yh + 1, c), [(0, 2)]))
-        put(2, 4 * c, product(g_left, gx_at(yh, c), [(2, 2)]))
+    put(1, 4 * (1 - core), product(g, p_right, [(0, 2)]))
     sum_near.send_x()
     sum_own.finish()
     for k in range(NYH):
@@ -231,20 +238,16 @@
     push(cells_of(g_opp, mine_q), f_opp, pair)
     arrived(cells_of(g_opp, 2 + mine_q), s_relay + 1)
     push(cells_of(g_opp, 2 + mine_q), f_opp + 1, pair)
-    l_right, l_left, l_relay, l_pair = slot(), slot(), slot(2), slot(4)
-    push(cells_of(g_right, 1 - right_q), l_relay, left)
-    push(cells_of(g_left, 3 - left_q), l_relay + 1, right)
-    push(cells_of(g, 0, 2), l_right, right, own(0, 2))
-    push(cells_of(g, 2, 2), l_left, left, own(2, 2))
     split_into(g_opp, mine_q, 1)
     split_into(g_opp, 2 + mine_q, 1)
     sum_near.send_z()
+    segments = [(mine_q, 1), (2 + mine_q, 1)]
+    put(3, 4 * core, product(gx_at(yh % 2, core), gx_at(yh % 2 + 2, core), segments))
     arrived(cells_of(p_opp, mine_q), f_opp)
     split_into(p_opp, mine_q, 1)
     arrived(cells_of(p_opp, 2 + mine_q), f_opp + 1)
     split_into(p_opp, 2 + mine_q, 1)
-    for c in range(2):
-        put(3, 4 * c, product(gx_at(yh % 2, core), gx_at(yh % 2 + 2, c), [(mine_q, 1), (2 + mine_q, 1)]))
+    put(3, 4 * (1 - core), product(gx_at(yh % 2, core), gx_at(yh % 2 + 2, 1 - core), segments))
     sum_opp.send_x()
     all_own.send_x()
     sum_near.send_y()
@@ -261,28 +264,28 @@
         f_ref[core, x, z, 2 * NYH + k] = (ysum[2 * k, 3] + ysum[2 * k + 1, 3]) + (ysum[2 * k + 4, 3] + ysum[2 * k + 5, 3])
     all_opp.send_z()
     all_near.send_x()
-    all_opp.send_x()
     arrived(cells_of(g_opp, far_q), l_relay)
     push(cells_of(g_opp, far_q), l_pair, pair)
     arrived(cells_of(g_opp, 2 + far_q), l_relay + 1)
     push(cells_of(g_opp, 2 + far_q), l_pair + 1, pair)
+    arrived(cells_of(g_left, 0, 2), l_right)
+    push(cells_of(g_left, 0, 2), l_pair + 2, pair)
+    arrived(cells_of(g_right, 2, 2), l_left)
+    push(cells_of(g_right, 2, 2), l_pair + 3, pair)
     split_into(g_opp, far_q, 1)
     split_into(g_opp, 2 + far_q, 1)
+    all_opp.send_x()
+    split_into(g_left, 0, 2)
+    split_into(g_right, 2, 2)
     arrived(cells_of(p_left, 2 + left_q), f_left)
     arrived(cells_of(p_left, 3 - left_q), f_left + 1)
     split_into(p_left, 2, 2)
     all_near.send_pair()
-    all_opp.send_pair()
-    arrived(cells_of(g_left, 0, 2), l_right)
-    push(cells_of(g_left, 0, 2), l_pair + 2, pair)
-    arrived(cells_of(g_right, 2, 2), l_left)
-    push(cells_of(g_right, 2, 2), l_pair + 3, pair)
-    split_into(g_left, 0, 2)
-    split_into(g_right, 2, 2)
     arrived(cells_of(p_opp, far_q), l_pair)
     split_into(p_opp, far_q, 1)
     arrived(cells_of(p_opp, 2 + far_q), l_pair + 1)
     split_into(p_opp, 2 + far_q, 1)
+    all_opp.send_pair()
     arrived(cells_of(p_left, 0, 2), l_pair + 2)
     split_into(p_left, 0, 2)
     arrived(cells_of(p_right, 2, 2), l_pair + 3)
@@ -414,7 +417,9 @@
             z_hi, z_lo = split2(jnp.concatenate(parts, axis=0))
             lanes = lax.broadcasted_iota(jnp.int32, (1, 256), 1)
             in_panel = (lanes >= p0) & (lanes < p0 + PANEL)
-            rest = jnp.where(in_panel, 0.0, below) - dot3(below[:, 128 * ct:128 * ct + 128], z_hi, z_lo)
+            cut = [below[:PANEL], below[PANEL:]] if below.shape[0] > PANEL else [below]
+            rest = jnp.concatenate([
+                jnp.where(in_panel, 0.0, v) - dot3(v[:, 128 * ct:128 * ct + 128], z_hi, z_lo) for v in cut], axis=0)
 
 
 def iterate_kernel(hi_ref, lo_ref, f_ref, start_ref, basis_ref, out_ref, g_hi, g_lo, i_ref, w_ref):

time: 121 us -> 126 us (1.041)
  Pallas kernels: 118 us -> 123 us
    pallas_call x1, Pallas kernels: 76.6 us -> 82.2 us  [gather_and_gram(): pl.pallas_call(functools.partial(gram_kernel, all_cells), out_shape=(jax....]
where the time goes in v4:
time: 126 us
  Pallas kernels  123 us (98%)
  local copies, waits for them, and re-layouts  2.16 us (2%)
    pallas_call x1, Pallas kernels, gather_and_gram(): pl.pallas_call(functools.partial(gram_kernel, all_cells), out_shape=(jax....  82.2 us
    pallas_call x1, Pallas kernels, iterate(): pl.pallas_call(iterate_kernel, out_shape=(jax.ShapeDtypeStruct((RANK, ROW...  41.2 us

profile of v4, /device:TPU:1, one launch (start us, length us, event | category | flops | bytes accessed | tf_op | source)
XLA Modules:
  0.0 126.2 jit_solution(7574342215968610260)
XLA Ops:
  0.6 0.0 copy-start.1
  0.6 1.0 copy-done.1
  1.7 82.2 %shard_map.41 = (bf16[8,128,1024]{2,1,0:T(8,128)(2,1)S(1)}, bf16[8,128,1024]{2,1,0:T(8,128)(2,1)S(1)}, f32[2,4,8,10,8,128]{5,4,3,2,1,0:T(8,128)S(1)}) custom-call(f32[128,1024]{1,0:T(8,128)S(1)} %copy-done.1), custom_call_target="tpu_custom_call" | custom-call | tf_op jit(solution)/shard_map/pallas_call | solution.py:306
  83.9 0.0 copy-start
  83.9 1.1 copy-done
  85.0 41.2 %shard_map.42 = (f32[192,128]{1,0:T(8,128)}, f32[128,1024]{1,0:T(8,128)}) custom-call(bf16[1024,1024]{1,0:T(8,128)(2,1)S(1)} %bitcast.4, bf16[1024,1024]{1,0:T(8,128)(2,1)S(1)} %bitcast.5, f32[2,4,8,10,8,128]{5,4,3,2,1,0:T(8,128)S(1)} %get-tuple-element.9.f_ref, f32[192,1024]{1,0:T(8,128)S(1)} %bitcast.6), custom_call_target="tpu_custom_call" | custom-call | tf_op jit(solution)/shard_map/pallas_call | solution.py:488
Async XLA Ops:
  0.6 1.0 copy-start.1
  83.9 1.1 copy-start

commit v5 on v4

--- a/solution.py
+++ b/solution.py
@@ -28,7 +28,7 @@
     return lax.dot_general(a, b, (((1,), (1,)), ((), ())), preferred_element_type=jnp.float32)
 
 
-def gram_kernel(cells, s_ref, hi_ref, lo_ref, f_ref, d_ref, parts, xin, xsum, zin, ysum, send, recv, local):
+def gram_kernel(cells, s_ref, hi_ref, lo_ref, f_ref, rest_right, rest_left, rest_opp, d_ref, parts, xin, xsum, zin, ysum, send, recv, local):
     g = lax.axis_index("gx")
     q = lax.axis_index("yz")
     yh, core = g // 2, g % 2
@@ -201,6 +201,17 @@
     for k in range(NX):
         parts[k, 0, 6:8] = jnp.zeros((2, 8, 128), f32)
     sum_own.send_x()
+    rest_right[...] = d_ref[g, :, :2 * quarter]
+    rest_left[...] = d_ref[g, :, 2 * quarter:]
+    rest_opp[:, :quarter] = d_ref[g, :, lanes(mine_q, 1)]
+    rest_opp[:, quarter:] = d_ref[g, :, lanes(2 + mine_q, 1)]
+    for block, gap in ((g_left, 0), (p_left, 0), (g_right, 2), (p_right, 2)):
+        hi_ref[block, :, lanes(gap, 2)] = jnp.zeros((ROWS, 2 * quarter), bf16)
+        lo_ref[block, :, lanes(gap, 2)] = jnp.zeros((ROWS, 2 * quarter), bf16)
+    for block in (g_opp, p_opp):
+        for gap in (far_q, 2 + far_q):
+            hi_ref[block, :, lanes(gap, 1)] = jnp.zeros((ROWS, quarter), bf16)
+            lo_ref[block, :, lanes(gap, 1)] = jnp.zeros((ROWS, quarter), bf16)
 
     arrived(cells_of(g_right, right_q), s_down)
     push(cells_of(g_right, right_q), s_relay, left)
@@ -213,11 +224,6 @@
     push(cells_of(g_right, 1 - right_q), f_right + 1, pair)
     arrived(cells_of(g_left, 3 - left_q), s_up + 1)
     push(cells_of(g_left, 3 - left_q), f_left + 1, pair)
-    l_right, l_left, l_relay, l_pair = slot(), slot(), slot(2), slot(4)
-    push(cells_of(g_right, 1 - right_q), l_relay, left)
-    push(cells_of(g_left, 3 - left_q), l_relay + 1, right)
-    push(cells_of(g, 0, 2), l_right, right, own(0, 2))
-    push(cells_of(g, 2, 2), l_left, left, own(2, 2))
     sum_own.send_y()
     split_into(g_right, 0, 2)
     split_into(g_left, 2, 2)
@@ -264,32 +270,12 @@
         f_ref[core, x, z, 2 * NYH + k] = (ysum[2 * k, 3] + ysum[2 * k + 1, 3]) + (ysum[2 * k + 4, 3] + ysum[2 * k + 5, 3])
     all_opp.send_z()
     all_near.send_x()
-    arrived(cells_of(g_opp, far_q), l_relay)
-    push(cells_of(g_opp, far_q), l_pair, pair)
-    arrived(cells_of(g_opp, 2 + far_q), l_relay + 1)
-    push(cells_of(g_opp, 2 + far_q), l_pair + 1, pair)
-    arrived(cells_of(g_left, 0, 2), l_right)
-    push(cells_of(g_left, 0, 2), l_pair + 2, pair)
-    arrived(cells_of(g_right, 2, 2), l_left)
-    push(cells_of(g_right, 2, 2), l_pair + 3, pair)
-    split_into(g_opp, far_q, 1)
-    split_into(g_opp, 2 + far_q, 1)
     all_opp.send_x()
-    split_into(g_left, 0, 2)
-    split_into(g_right, 2, 2)
     arrived(cells_of(p_left, 2 + left_q), f_left)
     arrived(cells_of(p_left, 3 - left_q), f_left + 1)
     split_into(p_left, 2, 2)
     all_near.send_pair()
-    arrived(cells_of(p_opp, far_q), l_pair)
-    split_into(p_opp, far_q, 1)
-    arrived(cells_of(p_opp, 2 + far_q), l_pair + 1)
-    split_into(p_opp, 2 + far_q, 1)
     all_opp.send_pair()
-    arrived(cells_of(p_left, 0, 2), l_pair + 2)
-    split_into(p_left, 0, 2)
-    arrived(cells_of(p_right, 2, 2), l_pair + 3)
-    split_into(p_right, 2, 2)
     for group in (all_own, all_near, all_opp):
         group.finish()
     for op in sent:
@@ -297,7 +283,7 @@
 
 
 TILES = 2 * NYH + 2
-SLOTS = 13 + 8 + 3 * (NX + NZ + NY) + 3 * (NZ + 2 * NX)
+SLOTS = 13 + 3 * (NX + NZ + NY) + 3 * (NZ + 2 * NX)
 
 
 def gather_and_gram(snapshot, all_cells):
@@ -307,9 +293,10 @@
         functools.partial(gram_kernel, all_cells),
         out_shape=(jax.ShapeDtypeStruct((G, ROWS, cols), bf16),
                    jax.ShapeDtypeStruct((G, ROWS, cols), bf16),
-                   jax.ShapeDtypeStruct((2, NX, NZ, TILES, 8, 128), f32)),
+                   jax.ShapeDtypeStruct((2, NX, NZ, TILES, 8, 128), f32),
+                   *[jax.ShapeDtypeStruct((ROWS, cols // 2), f32)] * 3),
         in_specs=[vmem],
-        out_specs=(vmem, vmem, vmem),
+        out_specs=(vmem,) * 6,
         scratch_shapes=[
             pltpu.VMEM((G, ROWS, cols), f32),
             pltpu.VMEM((NX, KINDS, NZ, 8, 128), f32),
@@ -422,8 +409,7 @@
                 jnp.where(in_panel, 0.0, v) - dot3(v[:, 128 * ct:128 * ct + 128], z_hi, z_lo) for v in cut], axis=0)
 
 
-def iterate_kernel(hi_ref, lo_ref, f_ref, start_ref, basis_ref, out_ref, g_hi, g_lo, i_ref, w_ref):
-    g = lax.axis_index("gx")
+def iterate_kernel(hi_ref, lo_ref, f_ref, start_ref, basis_ref, core_ref, g_hi, g_lo, i_ref, w_ref):
 
 
     def store(i, j, block):
@@ -476,10 +462,52 @@
     after = times(i_hi, i_lo, hi_ref[...], lo_ref[...])
     factor(i_hi, i_lo)
     w = w_ref[:, :RANK]
-    core = dot3(w, *split2(after))
-    mine_t = dot3(w, *split2(i_ref[:, pl.ds(pl.multiple_of(g * ROWS, ROWS), ROWS)]))
-    basis_ref[...] = mine_t
-    out_ref[...] = dot3(mine_t.T, *split2(core))
+    core_ref[...] = dot3(w, *split2(after))
+    basis_ref[...] = dot3(w, i_hi, i_lo)
+
+
+def project_kernel(basis_ref, core_ref, *refs):
+    near_refs, other_refs, (mine_ref, out_ref) = refs[:3], refs[3:6], refs[6:]
+    g = lax.axis_index("gx")
+    yh, c = g // 2, g % 2
+    half = near_refs[0].shape[1]
+
+    def term(k, ahead):
+        def of(ref, core):
+            block = (yh + ahead) % NYH * 2 + core
+            q = basis_ref[:, pl.ds(pl.multiple_of(block * ROWS, ROWS), ROWS)]
+            return dot3(q, *split2(ref[...]))
+        return of(near_refs[k], c) + of(other_refs[k], 1 - c)
+
+    left, right, opposite = term(0, 3), term(1, 1), term(2, 2)
+    far = 1 - yh // 2
+    quarter = half // 2
+    none = jnp.zeros((RANK, quarter), f32)
+    at_second = far == 1
+
+    def placed(piece):
+        first = jnp.concatenate([piece, none], axis=1)
+        second = jnp.concatenate([none, piece], axis=1)
+        return jnp.where(at_second, second, first)
+
+    low = core_ref[:, :half] + left + placed(opposite[:, :quarter])
+    high = core_ref[:, half:] + right + placed(opposite[:, quarter:])
+    mine_t = basis_ref[:, pl.ds(pl.multiple_of(g * ROWS, ROWS), ROWS)]
+    mine_ref[...] = mine_t
+    mine = mine_t.T
+    out_ref[:, :half] = dot3(mine, *split2(low))
+    out_ref[:, half:] = dot3(mine, *split2(high))
+
+
+def project(basis_t, core, near, other):
+    vmem = pl.BlockSpec(memory_space=pltpu.VMEM)
+    return pl.pallas_call(
+        project_kernel,
+        out_shape=(jax.ShapeDtypeStruct((RANK, ROWS), f32), jax.ShapeDtypeStruct((ROWS, core.shape[1]), f32)),
+        in_specs=[vmem] * 8,
+        out_specs=(vmem, vmem),
+        compiler_params=pltpu.CompilerParams(vmem_limit_bytes=16 * 2**20),
+    )(basis_t, core, *near, *other)
 
 
 def iterate(d_hi, d_lo, sums, start_t):
@@ -487,22 +515,28 @@
     vmem = pl.BlockSpec(memory_space=pltpu.VMEM)
     return pl.pallas_call(
         iterate_kernel,
-        out_shape=(jax.ShapeDtypeStruct((RANK, ROWS), f32), jax.ShapeDtypeStruct((ROWS, cols), f32)),
+        out_shape=(jax.ShapeDtypeStruct((RANK, N), f32), jax.ShapeDtypeStruct((RANK, cols), f32)),
         in_specs=[vmem] * 4,
         out_specs=(vmem, vmem),
         scratch_shapes=[
             pltpu.VMEM((N, N), bf16), pltpu.VMEM((N, N), bf16),
             pltpu.VMEM((RANK, N), f32), pltpu.VMEM((RANK, 256), f32)],
         compiler_params=pltpu.CompilerParams(vmem_limit_bytes=28 * 2**20),
+        cost_estimate=pl.CostEstimate(flops=40_000_000_000, bytes_accessed=120_000_000, transcendentals=0),
     )(d_hi, d_lo, sums, start_t)
 
 
 def body(snapshot, start):
     all_cells = snapshot.shape[1] * lax.axis_size("yz")
-    d_hi, d_lo, sums = gather_and_gram(snapshot, all_cells)
+    d_hi, d_lo, sums, *rest = gather_and_gram(snapshot, all_cells)
+    near = [lax.ppermute(r, "gx", [(i, (i + step) % G) for i in range(G)])
+            for r, step in zip(rest, (2, G - 2, G // 2))]
     shape = (N, snapshot.shape[1])
-    basis_t, projected = iterate(d_hi.reshape(shape), d_lo.reshape(shape), sums, start.T)
-    return basis_t.T, projected
+    basis_t, core = iterate(d_hi.reshape(shape), d_lo.reshape(shape), sums, start.T)
+    basis_t, core, *near = lax.optimization_barrier((basis_t, core, *near))
+    other = [lax.ppermute(r, "gx", [(i, i ^ 1) for i in range(G)]) for r in near]
+    mine_t, projected = project(basis_t, core, near, other)
+    return mine_t.T, projected
 
 
 def solution(mesh):

time: 126 us -> 133 us (1.056)
  starting transfers between devices: 0 us -> 19.3 us
  Pallas kernels: 123 us -> 110 us
    ppermute x0 -> x6, starting transfers between devices: none -> 19.3 us  [the longest x3 12.2 us: body(): lax.ppermute(r, 'gx', [(i, (i + step) % G) for i in range(G)])]
    pallas_call x1, Pallas kernels: 82.2 us -> 67.1 us  [gather_and_gram(): pl.pallas_call(functools.partial(gram_kernel, all_cells), out_shape=(jax....]
    pallas_call x1 -> x2, Pallas kernels: 41.2 us -> 42.4 us  [the longest x1 40.2 us: iterate(): pl.pallas_call(iterate_kernel, out_shape=(jax.ShapeDtypeStruct((RANK, N),...]
  transfers between devices with their start and end apart: 0 -> 6, of which waited for: 0 -> 1; matrix products, arithmetic and copies ran while one was open for 0% -> 0% of each run, Pallas kernels for 0% -> 30%
where the time goes in v5:
time: 133 us
  Pallas kernels  110 us (83%)
  starting transfers between devices  19.3 us (15%)
  local copies, waits for them, and re-layouts  2.16 us (2%)
    pallas_call x1, Pallas kernels, gather_and_gram(): pl.pallas_call(functools.partial(gram_kernel, all_cells), out_shape=(jax....  67.1 us
    pallas_call x1, Pallas kernels, iterate(): pl.pallas_call(iterate_kernel, out_shape=(jax.ShapeDtypeStruct((RANK, N),...  40.2 us
    ppermute x3, starting transfers between devices, body(): lax.ppermute(r, 'gx', [(i, (i + step) % G) for i in range(G)])  12.2 us
    ppermute x3, starting transfers between devices, body(): lax.ppermute(r, 'gx', [(i, i ^ 1) for i in range(G)])  7.05 us
  transfers between devices with their start and end apart: 6, of which 1 were waited for; matrix products, arithmetic and copies ran while one was open for 0% of the time, Pallas kernels for 30%

profile of v5, /device:TPU:1, one launch (start us, length us, event | category | flops | bytes accessed | tf_op | source)
XLA Modules:
  0.0 132.9 jit_solution(4615708208681050987)
XLA Ops:
  0.6 0.0 copy-start
  0.6 1.0 copy-done
  1.7 67.1 %shard_map.41 = (bf16[8,128,1024]{2,1,0:T(8,128)(2,1)S(1)}, bf16[8,128,1024]{2,1,0:T(8,128)(2,1)S(1)}, f32[2,4,8,10,8,128]{5,4,3,2,1,0:T(8,128)S(1)}, f32[128,51...) custom-call(f32[128,1024]{1,0:T(8,128)S(1)} %copy-done), custom_call_target="tpu_custom_call" | custom-call | tf_op jit(solution)/shard_map/pallas_call | solution.py:292
  68.8 3.9 %collective-permute-start = (f32[128,512]{1,0:T(8,128)S(1)}, f32[128,512]{1,0:T(8,128)S(1)}, u32[]{:S(2)}, u32[]{:S(2)}) collective-permute-start(f32[128,512]{1,0:T(8,128)S(1)} %get-tuple-element.22), channel_id=1, source_target_pairs={{0,128},{64,192},{128,256},{192,320},{256,384},{320,448},{384,0},{... | collective-permute-start | bytes 786440 | tf_op jit(solution)/shard_map/ppermute | solution.py:532
  72.7 3.5 %collective-permute-start.1 = (f32[128,512]{1,0:T(8,128)S(1)}, f32[128,512]{1,0:T(8,128)S(1)}, u32[]{:S(2)}, u32[]{:S(2)}) collective-permute-start(f32[128,512]{1,0:T(8,128)S(1)} %get-tuple-element.23), channel_id=1, source_target_pairs={{0,384},{64,448},{128,0},{192,64},{256,128},{320,192},{384,256},{4... | collective-permute-start | bytes 786440 | tf_op jit(solution)/shard_map/ppermute | solution.py:532
  76.2 4.8 %collective-permute-start.2 = (f32[128,512]{1,0:T(8,128)S(1)}, f32[128,512]{1,0:T(8,128)S(1)}, u32[]{:S(2)}, u32[]{:S(2)}) collective-permute-start(f32[128,512]{1,0:T(8,128)S(1)} %get-tuple-element.24), channel_id=1, source_target_pairs={{0,256},{64,320},{128,384},{192,448},{256,0},{320,64},{384,128},{4... | collective-permute-start | bytes 786440 | tf_op jit(solution)/shard_map/ppermute | solution.py:532
  81.1 0.0 copy-start.1
  81.1 1.1 copy-done.1
  82.2 40.2 %shard_map.42 = (f32[192,1024]{1,0:T(8,128)S(1)}, f32[192,1024]{1,0:T(8,128)S(1)}) custom-call(bf16[1024,1024]{1,0:T(8,128)(2,1)S(1)} %bitcast.4, bf16[1024,1024]{1,0:T(8,128)(2,1)S(1)} %bitcast.5, f32[2,4,8,10,8,128]{5,4,3,2,1,0:T(8,128)S(1)} %get-tuple-element.19.f_ref, f32[192,1024]{1,0:T(8,128)S(1)} %bitcast.6), custom_call_target="tpu_custom_call" | custom-call | flops 40000000000 | bytes 120000000 | tf_op jit(solution)/shard_map/pallas_call | solution.py:516
  122.4 0.0 collective-permute-done.refs_0_
  122.4 0.0 collective-permute-done.1.refs_1_
  122.4 0.0 collective-permute-done.2.refs_2_
  122.4 2.7 %collective-permute-start.3 = (f32[128,512]{1,0:T(8,128)S(1)}, f32[128,512]{1,0:T(8,128)S(1)}, u32[]{:S(2)}, u32[]{:S(2)}) collective-permute-start(f32[128,512]{1,0:T(8,128)S(1)} %collective-permute-done.refs_0_), channel_id=1, source_target_pairs={{0,64},{64,0},{128,192},{192,128},{256,320},{320,256},{384,448},{4... | collective-permute-start | bytes 786440 | tf_op jit(solution)/shard_map/ppermute | solution.py:537
  125.2 1.9 %collective-permute-start.4 = (f32[128,512]{1,0:T(8,128)S(1)}, f32[128,512]{1,0:T(8,128)S(1)}, u32[]{:S(2)}, u32[]{:S(2)}) collective-permute-start(f32[128,512]{1,0:T(8,128)S(1)} %collective-permute-done.1.refs_1_), channel_id=1, source_target_pairs={{0,64},{64,0},{128,192},{192,128},{256,320},{320,256},{384,448},{4... | collective-permute-start | bytes 786440 | tf_op jit(solution)/shard_map/ppermute | solution.py:537
  127.1 2.4 %collective-permute-start.5 = (f32[128,512]{1,0:T(8,128)S(1)}, f32[128,512]{1,0:T(8,128)S(1)}, u32[]{:S(2)}, u32[]{:S(2)}) collective-permute-start(f32[128,512]{1,0:T(8,128)S(1)} %collective-permute-done.2.refs_2_), channel_id=1, source_target_pairs={{0,64},{64,0},{128,192},{192,128},{256,320},{320,256},{384,448},{4... | collective-permute-start | bytes 786440 | tf_op jit(solution)/shard_map/ppermute | solution.py:537
  129.5 0.0 collective-permute-done.3.refs_3_
  129.5 0.0 collective-permute-done.4.refs_4_
  129.5 1.1 collective-permute-done.5.refs_5_
  130.6 2.2 %shard_map.43 = (f32[192,128]{1,0:T(8,128)}, f32[128,1024]{1,0:T(8,128)}) custom-call(f32[192,1024]{1,0:T(8,128)S(1)} %get-tuple-element.25.basis_ref, f32[192,1024]{1,0:T(8,128)S(1)} %get-tuple-element.26.core_ref, f32[128,512]{1,0:T(8,128)S(1)} %collective-permute-done.refs_0_, f32[128,512]{1,0:T(8,128)S(1)} %collective-permute-done.1.refs_1_, ...), custom_call_target="tpu_custom_call" | custom-call | tf_op jit(solution)/shard_map/pallas_call | solution.py:504
Async XLA Ops:
  0.6 1.0 copy-start
  68.8 53.6 %collective-permute-start = (f32[128,512]{1,0:T(8,128)S(1)}, f32[128,512]{1,0:T(8,128)S(1)}, u32[]{:S(2)}, u32[]{:S(2)}) collective-permute-start(f32[128,512]{1,0:T(8,128)S(1)} %get-tuple-element.22), channel_id=1, source_target_pairs={{0,128},{64,192},{128,256},{192,320},{256,384},{320,448},{384,0},{... | collective-permute-start | bytes 786440 | tf_op jit(solution)/shard_map/ppermute | solution.py:532
  72.7 49.7 %collective-permute-start.1 = (f32[128,512]{1,0:T(8,128)S(1)}, f32[128,512]{1,0:T(8,128)S(1)}, u32[]{:S(2)}, u32[]{:S(2)}) collective-permute-start(f32[128,512]{1,0:T(8,128)S(1)} %get-tuple-element.23), channel_id=1, source_target_pairs={{0,384},{64,448},{128,0},{192,64},{256,128},{320,192},{384,256},{4... | collective-permute-start | bytes 786440 | tf_op jit(solution)/shard_map/ppermute | solution.py:532
  76.2 46.2 %collective-permute-start.2 = (f32[128,512]{1,0:T(8,128)S(1)}, f32[128,512]{1,0:T(8,128)S(1)}, u32[]{:S(2)}, u32[]{:S(2)}) collective-permute-start(f32[128,512]{1,0:T(8,128)S(1)} %get-tuple-element.24), channel_id=1, source_target_pairs={{0,256},{64,320},{128,384},{192,448},{256,0},{320,64},{384,128},{4... | collective-permute-start | bytes 786440 | tf_op jit(solution)/shard_map/ppermute | solution.py:532
  81.1 1.1 copy-start.1
  122.4 7.1 %collective-permute-start.3 = (f32[128,512]{1,0:T(8,128)S(1)}, f32[128,512]{1,0:T(8,128)S(1)}, u32[]{:S(2)}, u32[]{:S(2)}) collective-permute-start(f32[128,512]{1,0:T(8,128)S(1)} %collective-permute-done.refs_0_), channel_id=1, source_target_pairs={{0,64},{64,0},{128,192},{192,128},{256,320},{320,256},{384,448},{4... | collective-permute-start | bytes 786440 | tf_op jit(solution)/shard_map/ppermute | solution.py:537
  125.2 4.4 %collective-permute-start.4 = (f32[128,512]{1,0:T(8,128)S(1)}, f32[128,512]{1,0:T(8,128)S(1)}, u32[]{:S(2)}, u32[]{:S(2)}) collective-permute-start(f32[128,512]{1,0:T(8,128)S(1)} %collective-permute-done.1.refs_1_), channel_id=1, source_target_pairs={{0,64},{64,0},{128,192},{192,128},{256,320},{320,256},{384,448},{4... | collective-permute-start | bytes 786440 | tf_op jit(solution)/shard_map/ppermute | solution.py:537
  127.1 3.6 %collective-permute-start.5 = (f32[128,512]{1,0:T(8,128)S(1)}, f32[128,512]{1,0:T(8,128)S(1)}, u32[]{:S(2)}, u32[]{:S(2)}) collective-permute-start(f32[128,512]{1,0:T(8,128)S(1)} %collective-permute-done.2.refs_2_), channel_id=1, source_target_pairs={{0,64},{64,0},{128,192},{192,128},{256,320},{320,256},{384,448},{4... | collective-permute-start | bytes 786440 | tf_op jit(solution)/shard_map/ppermute | solution.py:537

commit v6 on v4

--- a/solution.py
+++ b/solution.py
@@ -213,11 +213,6 @@
     push(cells_of(g_right, 1 - right_q), f_right + 1, pair)
     arrived(cells_of(g_left, 3 - left_q), s_up + 1)
     push(cells_of(g_left, 3 - left_q), f_left + 1, pair)
-    l_right, l_left, l_relay, l_pair = slot(), slot(), slot(2), slot(4)
-    push(cells_of(g_right, 1 - right_q), l_relay, left)
-    push(cells_of(g_left, 3 - left_q), l_relay + 1, right)
-    push(cells_of(g, 0, 2), l_right, right, own(0, 2))
-    push(cells_of(g, 2, 2), l_left, left, own(2, 2))
     sum_own.send_y()
     split_into(g_right, 0, 2)
     split_into(g_left, 2, 2)
@@ -229,6 +224,9 @@
     split_into(p_right, 0, 2)
     put(1, 4 * (1 - core), product(g, p_right, [(0, 2)]))
     sum_near.send_x()
+    l_right, l_left, l_relay, l_pair = slot(2), slot(2), slot(2), slot(6)
+    push(cells_of(g_right, 1 - right_q), l_relay, left)
+    push(cells_of(g_left, 3 - left_q), l_relay + 1, right)
     sum_own.finish()
     for k in range(NYH):
         f_ref[core, x, z, k] = ysum[2 * k, 0] + ysum[2 * k + 1, 0]
@@ -238,6 +236,8 @@
     push(cells_of(g_opp, mine_q), f_opp, pair)
     arrived(cells_of(g_opp, 2 + mine_q), s_relay + 1)
     push(cells_of(g_opp, 2 + mine_q), f_opp + 1, pair)
+    push(cells_of(g, 0), l_right, right, own(0))
+    push(cells_of(g, 2), l_left, left, own(2))
     split_into(g_opp, mine_q, 1)
     split_into(g_opp, 2 + mine_q, 1)
     sum_near.send_z()
@@ -258,37 +258,43 @@
         f_ref[core, x, z, NYH + k] = (ysum[2 * k, 1] + ysum[2 * k + 1, 1]) + (ysum[2 * after, 2] + ysum[2 * after + 1, 2])
     all_near.send_z()
     sum_opp.send_y()
+    push(cells_of(g, 1), l_right + 1, right, own(1))
+    push(cells_of(g, 3), l_left + 1, left, own(3))
     all_own.send_pair()
     sum_opp.finish()
     for k in range(2):
         f_ref[core, x, z, 2 * NYH + k] = (ysum[2 * k, 3] + ysum[2 * k + 1, 3]) + (ysum[2 * k + 4, 3] + ysum[2 * k + 5, 3])
     all_opp.send_z()
     all_near.send_x()
-    arrived(cells_of(g_opp, far_q), l_relay)
-    push(cells_of(g_opp, far_q), l_pair, pair)
-    arrived(cells_of(g_opp, 2 + far_q), l_relay + 1)
-    push(cells_of(g_opp, 2 + far_q), l_pair + 1, pair)
-    arrived(cells_of(g_left, 0, 2), l_right)
-    push(cells_of(g_left, 0, 2), l_pair + 2, pair)
-    arrived(cells_of(g_right, 2, 2), l_left)
-    push(cells_of(g_right, 2, 2), l_pair + 3, pair)
+    for k in range(2):
+        arrived(cells_of(g_opp, 2 * k + far_q), l_relay + k)
+        push(cells_of(g_opp, 2 * k + far_q), l_pair + k, pair)
+    arrived(cells_of(g_left, 0), l_right)
+    push(cells_of(g_left, 0), l_pair + 2, pair)
+    arrived(cells_of(g_right, 2), l_left)
+    push(cells_of(g_right, 2), l_pair + 3, pair)
     split_into(g_opp, far_q, 1)
     split_into(g_opp, 2 + far_q, 1)
     all_opp.send_x()
-    split_into(g_left, 0, 2)
-    split_into(g_right, 2, 2)
     arrived(cells_of(p_left, 2 + left_q), f_left)
     arrived(cells_of(p_left, 3 - left_q), f_left + 1)
     split_into(p_left, 2, 2)
     all_near.send_pair()
-    arrived(cells_of(p_opp, far_q), l_pair)
-    split_into(p_opp, far_q, 1)
-    arrived(cells_of(p_opp, 2 + far_q), l_pair + 1)
-    split_into(p_opp, 2 + far_q, 1)
+    for k in range(2):
+        arrived(cells_of(p_opp, 2 * k + far_q), l_pair + k)
+        split_into(p_opp, 2 * k + far_q, 1)
     all_opp.send_pair()
-    arrived(cells_of(p_left, 0, 2), l_pair + 2)
+    arrived(cells_of(g_left, 1), l_right + 1)
+    push(cells_of(g_left, 1), l_pair + 4, pair)
+    arrived(cells_of(g_right, 3), l_left + 1)
+    push(cells_of(g_right, 3), l_pair + 5, pair)
+    split_into(g_left, 0, 2)
+    split_into(g_right, 2, 2)
+    arrived(cells_of(p_left, 0), l_pair + 2)
+    arrived(cells_of(p_left, 1), l_pair + 4)
     split_into(p_left, 0, 2)
-    arrived(cells_of(p_right, 2, 2), l_pair + 3)
+    arrived(cells_of(p_right, 2), l_pair + 3)
+    arrived(cells_of(p_right, 3), l_pair + 5)
     split_into(p_right, 2, 2)
     for group in (all_own, all_near, all_opp):
         group.finish()
@@ -297,7 +303,7 @@
 
 
 TILES = 2 * NYH + 2
-SLOTS = 13 + 8 + 3 * (NX + NZ + NY) + 3 * (NZ + 2 * NX)
+SLOTS = 13 + 12 + 3 * (NX + NZ + NY) + 3 * (NZ + 2 * NX)
 
 
 def gather_and_gram(snapshot, all_cells):

time: 126 us -> 113 us (0.90)
  Pallas kernels: 123 us -> 110 us
    pallas_call x1, Pallas kernels: 82.2 us -> 68.8 us  [gather_and_gram(): pl.pallas_call(functools.partial(gram_kernel, all_cells), out_shape=(jax....]
where the time goes in v6:
time: 113 us
  Pallas kernels  110 us (97%)
  local copies, waits for them, and re-layouts  2.16 us (2%)
    pallas_call x1, Pallas kernels, gather_and_gram(): pl.pallas_call(functools.partial(gram_kernel, all_cells), out_shape=(jax....  68.8 us
    pallas_call x1, Pallas kernels, iterate(): pl.pallas_call(iterate_kernel, out_shape=(jax.ShapeDtypeStruct((RANK, ROW...  41.2 us

profile of v6, /device:TPU:1, one launch (start us, length us, event | category | flops | bytes accessed | tf_op | source)
XLA Modules:
  0.0 112.8 jit_solution(4610552982833207733)
XLA Ops:
  0.6 0.0 copy-start.1
  0.6 1.0 copy-done.1
  1.7 68.8 %shard_map.41 = (bf16[8,128,1024]{2,1,0:T(8,128)(2,1)S(1)}, bf16[8,128,1024]{2,1,0:T(8,128)(2,1)S(1)}, f32[2,4,8,10,8,128]{5,4,3,2,1,0:T(8,128)S(1)}) custom-call(f32[128,1024]{1,0:T(8,128)S(1)} %copy-done.1), custom_call_target="tpu_custom_call" | custom-call | tf_op jit(solution)/shard_map/pallas_call | solution.py:312
  70.5 0.0 copy-start
  70.5 1.1 copy-done
  71.6 41.2 %shard_map.42 = (f32[192,128]{1,0:T(8,128)}, f32[128,1024]{1,0:T(8,128)}) custom-call(bf16[1024,1024]{1,0:T(8,128)(2,1)S(1)} %bitcast.4, bf16[1024,1024]{1,0:T(8,128)(2,1)S(1)} %bitcast.5, f32[2,4,8,10,8,128]{5,4,3,2,1,0:T(8,128)S(1)} %get-tuple-element.9.f_ref, f32[192,1024]{1,0:T(8,128)S(1)} %bitcast.6), custom_call_target="tpu_custom_call" | custom-call | tf_op jit(solution)/shard_map/pallas_call | solution.py:494
Async XLA Ops:
  0.6 1.0 copy-start.1
  70.5 1.1 %copy-start = (f32[1024,192]{0,1:T(8,128)S(1)}, f32[1024,192]{0,1:T(8,128)}, u32[]{:S(2)}) copy-start(f32[1024,192]{0,1:T(8,128)} %param.3) | copy-start | bytes 2359300

commit v7 on v6

--- a/solution.py
+++ b/solution.py
@@ -345,8 +345,7 @@
 
 
 def reciprocal(x):
-    r = pl.reciprocal(x, approx=True)
-    return r * (2.0 - x * r)
+    return pl.reciprocal(x, approx=True)
 
 
 def inverse_factor(m, w_ref):

time: 113 us -> 112 us (level)
  no operation moved by 1% of the time
where the time goes in v7:
time: 112 us
  Pallas kernels  109 us (97%)
  local copies, waits for them, and re-layouts  2.16 us (2%)
    pallas_call x1, Pallas kernels, gather_and_gram(): pl.pallas_call(functools.partial(gram_kernel, all_cells), out_shape=(jax....  68.8 us
    pallas_call x1, Pallas kernels, iterate(): pl.pallas_call(iterate_kernel, out_shape=(jax.ShapeDtypeStruct((RANK, ROW...  40.3 us

profile of v7, /device:TPU:1, one launch (start us, length us, event | category | flops | bytes accessed | tf_op | source)
XLA Modules:
  0.0 111.9 jit_solution(10522382236965474870)
XLA Ops:
  0.6 0.0 copy-start.1
  0.6 1.0 copy-done.1
  1.7 68.8 %shard_map.41 = (bf16[8,128,1024]{2,1,0:T(8,128)(2,1)S(1)}, bf16[8,128,1024]{2,1,0:T(8,128)(2,1)S(1)}, f32[2,4,8,10,8,128]{5,4,3,2,1,0:T(8,128)S(1)}) custom-call(f32[128,1024]{1,0:T(8,128)S(1)} %copy-done.1), custom_call_target="tpu_custom_call" | custom-call | tf_op jit(solution)/shard_map/pallas_call | solution.py:312
  70.5 0.0 copy-start
  70.5 1.1 %copy-done = f32[1024,192]{0,1:T(8,128)S(1)} copy-done((f32[1024,192]{0,1:T(8,128)S(1)}, f32[1024,192]{0,1:T(8,128)}, u32[]{:S(2)}) %copy-start) | copy-done | bytes 786456
  71.6 40.3 %shard_map.42 = (f32[192,128]{1,0:T(8,128)}, f32[128,1024]{1,0:T(8,128)}) custom-call(bf16[1024,1024]{1,0:T(8,128)(2,1)S(1)} %bitcast.4, bf16[1024,1024]{1,0:T(8,128)(2,1)S(1)} %bitcast.5, f32[2,4,8,10,8,128]{5,4,3,2,1,0:T(8,128)S(1)} %get-tuple-element.9.f_ref, f32[192,1024]{1,0:T(8,128)S(1)} %bitcast.6), custom_call_target="tpu_custom_call" | custom-call | tf_op jit(solution)/shard_map/pallas_call | solution.py:493
Async XLA Ops:
  0.6 1.0 copy-start.1
  70.5 1.1 %copy-start = (f32[1024,192]{0,1:T(8,128)S(1)}, f32[1024,192]{0,1:T(8,128)}, u32[]{:S(2)}) copy-start(f32[1024,192]{0,1:T(8,128)} %param.3) | copy-start | bytes 2359300
